TPU v7x, 256 devices: a whole 4x4x8 slice. The times are simulated.
256 devices in a mesh: img: 32 (over z, x), txt: 8 (over y, core).
Axes of the slice: x: 4, y: 4, z: 8, core: 2. Of those that a mesh axis runs over, the one named last changes fastest.
Arguments:
- picture_vectors: float32 [16384, 1152], P(('img', 'txt')), may hold values from -0.2 to 0.2
- caption_vectors: float32 [16384, 1152], P(('txt', 'img')), may hold values from -0.2 to 0.2
- warmth_exponent: float32 [1], replicated, may hold values from 3 to 3.7
- offset_weight: float32 [1], replicated, may hold values from -8 to -5
Outputs:
- mean_sigmoid_penalty: float32 [1], replicated
- picture_derivative: float32 [16384, 1152], P(('img', 'txt'))
- caption_derivative: float32 [16384, 1152], P(('txt', 'img'))
- warmth_derivative: float32 [1], replicated
- offset_derivative: float32 [1], replicated
All inputs are finite; a program needn't handle non-finite values.
Results may differ from a plain program's by a relative error of at most 0.0003.
Values sent between devices are 32-bit elements; how exact they have to be, the bound alone decides.
A program may use at most 128 MiB of HBM per device.

v0:
```python
import jax
import jax.numpy as jnp
from jax import lax
from jax.sharding import PartitionSpec as P


def unit_rows(values):
    row_norm = jnp.sqrt(jnp.sum(values * values, axis=1, keepdims=True) + 1e-06)
    return (values / row_norm, row_norm)


def project_back(unit, row_norm, grads):
    inner = jnp.sum(unit * grads, axis=1, keepdims=True)
    return (grads - unit * inner) / row_norm


def body(picture_vectors, caption_vectors, warmth_exponent, offset_weight):
    full_accuracy_mode = lax.Precision.HIGHEST
    shard_rows = picture_vectors.shape[0]
    image_block = lax.all_gather(picture_vectors, "txt", axis=0, tiled=True)
    text_block = lax.all_gather(caption_vectors, "img", axis=0, tiled=True)
    image_unit, image_norm = unit_rows(image_block)
    caption_unitlength, text_norm = unit_rows(text_block)
    image_count = image_block.shape[0]
    text_count = text_block.shape[0]
    matched_examples = shard_rows * lax.axis_size("img") * lax.axis_size("txt")
    image_start = lax.axis_index("img") * image_count
    text_start = lax.axis_index("txt") * text_count
    warmth_multiplier = jnp.exp(warmth_exponent[0])
    rotation_offset = offset_weight[0]
    cosine_affinity_grid = jnp.dot(
        image_unit,
        caption_unitlength.T,
        precision=full_accuracy_mode,
        preferred_element_type=jnp.float32,
    )
    pairwise_energy_grid = warmth_multiplier * cosine_affinity_grid + rotation_offset
    row_ids = image_start + lax.broadcasted_iota(jnp.int32, (image_count, text_count), 0)
    column_ids = text_start + lax.broadcasted_iota(jnp.int32, (image_count, text_count), 1)
    labels = jnp.where(row_ids == column_ids, 1.0, -1.0).astype(jnp.float32)
    losses = jax.nn.softplus(-labels * pairwise_energy_grid)
    energy_derivative_grid = -labels * jax.nn.sigmoid(-labels * pairwise_energy_grid)
    local_loss = jnp.sum(losses)
    warmth_replica = jnp.sum(energy_derivative_grid * cosine_affinity_grid)
    offset_replica = jnp.sum(energy_derivative_grid)
    penalty_accrued = lax.psum(local_loss, ("img", "txt"))
    image_own = lax.axis_index("txt") * shard_rows
    text_own = lax.axis_index("img") * shard_rows
    piece = energy_derivative_grid
    image_part = lax.psum_scatter(
        warmth_multiplier
        * jnp.dot(
            piece,
            caption_unitlength,
            precision=full_accuracy_mode,
            preferred_element_type=jnp.float32,
        ),
        "txt",
        scatter_dimension=0,
        tiled=True,
    )
    piece = energy_derivative_grid
    text_part = lax.psum_scatter(
        warmth_multiplier
        * jnp.dot(
            piece.T, image_unit, precision=full_accuracy_mode, preferred_element_type=jnp.float32
        ),
        "img",
        scatter_dimension=0,
        tiled=True,
    )
    own_image = lax.dynamic_slice_in_dim(image_unit, image_own, shard_rows, 0)
    own_image_norm = lax.dynamic_slice_in_dim(image_norm, image_own, shard_rows, 0)
    picture_derivative = project_back(own_image, own_image_norm, image_part)
    own_text = lax.dynamic_slice_in_dim(caption_unitlength, text_own, shard_rows, 0)
    own_text_norm = lax.dynamic_slice_in_dim(text_norm, text_own, shard_rows, 0)
    caption_derivative = project_back(own_text, own_text_norm, text_part)
    warmth_accrued, offset_accrued = lax.psum((warmth_replica, offset_replica), ("img", "txt"))
    mean_sigmoid_penalty = (penalty_accrued / matched_examples).reshape(1)
    warmth_derivative = (warmth_multiplier * warmth_accrued / matched_examples).reshape(1)
    offset_derivative = (offset_accrued / matched_examples).reshape(1)
    return (
        mean_sigmoid_penalty,
        picture_derivative,
        caption_derivative,
        warmth_derivative,
        offset_derivative,
    )


def solution(mesh):
    in_specs = (P(("img", "txt"), None), P(("txt", "img"), None), P(), P())
    out_specs = (P(), P(("img", "txt"), None), P(("txt", "img"), None), P(), P())
    return jax.shard_map(body, mesh=mesh, in_specs=in_specs, out_specs=out_specs, check_vma=False)
```

profile of v0, /device:TPU:1, one launch (start us, length us, event | category | flops | bytes accessed | tf_op | source)
XLA Modules:
  0.0 482.9 jit_solution(2187389076383404200)
XLA Ops:
  7.2 0.0 all-gather.3.cloned.1.call-start
  7.2 0.7 all-gather.3.cloned.1.call-update
  7.9 0.0 all-gather.5.cloned.1.call-start
  7.9 0.7 all-gather.5.cloned.1.call-update
  8.6 0.0 reduce-scatter.3.cloned.1.call-start
  10.1 32.2 %all-gather.3.cloned.1.call-done = f32[512,1152]{1,0:T(8,128)} async-done(((f32[64,1152]{1,0:T(8,128)}), f32[512,1152]{1,0:T(8,128)}) %all-gather.3.cloned.1.call-update) | async-done | bytes 2359312 | tf_op jit(solution)/shard_map/all_gather | solution.py:20
  42.3 1.9 multiply_reduce_fusion.2
  44.2 1.9 broadcast_divide_fusion.1
  46.1 102.0 %all-gather.5.cloned.1.call-done = f32[2048,1152]{1,0:T(8,128)} async-done(((f32[64,1152]{1,0:T(8,128)}), f32[2048,1152]{1,0:T(8,128)}) %all-gather.5.cloned.1.call-update) | async-done | bytes 9437200 | tf_op jit(solution)/shard_map/all_gather | solution.py:21
  148.1 0.0 copy-start
  148.1 4.5 multiply_reduce_fusion
  152.6 1.8 copy-done
  154.5 4.5 broadcast_divide_fusion
  158.9 0.0 copy-start.1
  158.9 24.8 %fusion.1 = (f32[]{:T(128)}, f32[]{:T(128)}, f32[]{:T(128)}, f32[512,2048]{1,0:T(8,128)S(1)}) fusion(f32[]{:T(128)} %bitcast.11, f32[]{:T(128)} %bitcast, s32[2048]{0:T(1024)S(1)} %iota_add_fusion, s32[512]{0:T(512)S(1)} %iota_add_fusion.1, f32[512,1152]{1,0:T(8,128)S(1)} %broadcast_divide_fusion.1, f32[2048,1152]{1,0:T(8,128)} %broadcast_divide_fusion), kind=kOutput, calls=%fused_computation.20 | convolution fusion | flops 14516486144 | bytes 16001044 | tf_op jit(solution)/shard_map/dot_general | solution.py:31
  183.7 0.0 copy-start.2
  183.7 2.0 copy-done.2
  185.7 0.0 copy-done.1
  185.7 19.8 %convolution_multiply_fusion.1 = f32[512,1152]{1,0:T(8,128)} fusion(f32[2048,1152]{1,0:T(8,128)S(1)} %copy-done.1, f32[]{:T(128)} %bitcast, f32[512,2048]{1,0:T(8,128)S(1)} %get-tuple-element.11, f32[]{:T(128)} %bitcast.9, s32[2048]{0:T(1024)S(1)} %iota_add_fusion, s32[512]{0:T(512)S(1)} %iota_add_fusion.1), kind=kOutput, calls=%fused_computation.9 | convolution fusion | flops 14506590208 | bytes 16001032 | tf_op jit(solution)/shard_map/dot_general | solution.py:52
  205.5 0.0 reduce-scatter.3.cloned.1.call-update
  205.5 0.0 reduce-scatter.5.cloned.1.call-start
  205.6 22.0 %convolution_multiply_fusion = f32[2048,1152]{1,0:T(8,128)} fusion(f32[512,1152]{1,0:T(8,128)S(1)} %broadcast_divide_fusion.1, f32[]{:T(128)} %bitcast, f32[512,2048]{1,0:T(8,128)} %copy-done.2, f32[]{:T(128)} %bitcast.10, s32[2048]{0:T(1024)S(1)} %iota_add_fusion, s32[512]{0:T(512)S(1)} %iota_add_fusion.1), kind=kOutput, calls=%fused_computation.1 | convolution fusion | flops 14508359680 | bytes 16001032 | tf_op jit(solution)/shard_map/dot_general | solution.py:65
  227.6 0.0 reduce-scatter.5.cloned.1.call-update
  227.6 0.1 dynamic-slice.6
  227.7 76.2 %all-reduce = (f32[]{:T(128)}, f32[]{:T(128)}, f32[]{:T(128)}) all-reduce(f32[]{:T(128)} %get-tuple-element.7, f32[]{:T(128)} %get-tuple-element.6, f32[]{:T(128)} %get-tuple-element.5), channel_id=1, replica_groups=mesh['img'=32,'txt'=8] {'img','txt'}, use_global_device_ids=true, to_apply=%region_3.4 | all-reduce | flops 3 | bytes 24 | tf_op jit(solution)/shard_map/psum | solution.py:46
  303.9 0.1 dynamic-slice.7
  305.9 0.0 reduce-scatter.3.cloned.1.call-done
  305.9 1.1 multiply_reduce_fusion.4
  307.0 1.8 subtract_divide_fusion.1
  308.8 160.9 %reduce-scatter.5.cloned.1.call-done = f32[64,1152]{1,0:T(8,128)} async-done(((f32[2048,1152]{1,0:T(8,128)}), f32[64,1152]{1,0:T(8,128)}) %reduce-scatter.5.cloned.1.call-update) | async-done | bytes 294928 | tf_op jit(solution)/shard_map/reduce_scatter | solution.py:63
  469.7 1.2 multiply_reduce_fusion.3
  470.9 1.9 subtract_divide_fusion
  (4 shorter events, 0.0 us)
Async XLA Ops:
  7.2 35.1 %all-gather.3.cloned.1.call-start = ((), (), s32[]{:S(2)}) async-start(), calls=%async_computation.2 | async-start | bytes 2654208 | tf_op jit(solution)/shard_map/all_gather | solution.py:20
  7.9 140.2 %all-gather.5.cloned.1.call-start = ((), (), s32[]{:S(2)}) async-start(), calls=%async_computation.3 | async-start | bytes 9732096 | tf_op jit(solution)/shard_map/all_gather | solution.py:21
  8.6 297.3 %reduce-scatter.3.cloned.1.call-start = ((), (), s32[]{:S(2)}) async-start(), calls=%async_computation.4 | async-start | bytes 2654208 | tf_op jit(solution)/shard_map/reduce_scatter | solution.py:50
  148.1 6.4 %copy-start = (f32[2048,1152]{1,0:T(8,128)S(1)}, f32[2048,1152]{1,0:T(8,128)}, u32[]{:S(2)}) copy-start(f32[2048,1152]{1,0:T(8,128)} %all-gather.5.cloned.1.call-done) | copy-start | bytes 28311556
  158.9 26.8 %copy-start.1 = (f32[2048,1152]{1,0:T(8,128)S(1)}, f32[2048,1152]{1,0:T(8,128)}, u32[]{:S(2)}) copy-start(f32[2048,1152]{1,0:T(8,128)} %broadcast_divide_fusion) | copy-start | bytes 28311556
  183.7 2.0 copy-start.2
  205.5 264.2 %reduce-scatter.5.cloned.1.call-start = ((), (), s32[]{:S(2)}) async-start(), calls=%async_computation.5 | async-start | bytes 9732096 | tf_op jit(solution)/shard_map/reduce_scatter | solution.py:63
Sparse Core Ops, SparseCore 0:
  9.8 32.3 all-gather.2
  44.8 103.1 all-gather.4
  205.7 31.5 reduce-scatter.2
  241.2 228.4 reduce-scatter.4
where the time goes:
time: 489 us; the launch traced here: 483 us
  waiting for transfers between devices  297 us (61%)
  blocking collectives  76.2 us (16%)
  matrix products  66.5 us (14%)
  between operations  20.7 us (4%)
  other arithmetic  18.8 us (4%)
    reduce_scatter x1, waiting for transfers between devices, body(): lax.psum_scatter(warmth_multiplier * jnp.dot(piece.T, image_unit, precisi...  161 us
    all_gather x1, waiting for transfers between devices, body(): text_block = lax.all_gather(caption_vectors, 'img', axis=0, tiled=True)  102 us
    psum x1, blocking collectives, body(): penalty_accrued = lax.psum(local_loss, ('img', 'txt'))  76.2 us
    all_gather x1, waiting for transfers between devices, body(): image_block = lax.all_gather(picture_vectors, 'txt', axis=0, tiled=True)  32.2 us
    dot_general x1, matrix products, body(): jnp.dot(image_unit, caption_unitlength.T, precision=full_accuracy_mode, p...  24.8 us
    dot_general x1, matrix products, body(): jnp.dot(piece.T, image_unit, precision=full_accuracy_mode, preferred_elem...  22 us
    dot_general x1, matrix products, body(): jnp.dot(piece, caption_unitlength, precision=full_accuracy_mode, preferre...  19.8 us
  transfers between devices with their start and end apart: 4, of which 3 were waited for; matrix products, arithmetic and copies ran while one was open for 6% of the time, Pallas kernels for 0%

commit v1 on v0

v1 whole, which is shorter than its diff:
```python
import functools

import jax
import jax.numpy as jnp
from jax import lax
from jax.experimental import pallas as pl
from jax.experimental.pallas import tpu as pltpu
from jax.sharding import PartitionSpec as P

MESH = pl.DeviceIdType.MESH
F32, BF16 = jnp.float32, jnp.bfloat16
NX, NY, NZ = 4, 4, 8
SHARD, HALF, QUARTER, D = 64, 32, 16, 1152
ROWS = 1024
TI, TT = 256, 512
NT = (((1,), (1,)), ((), ()))
NN = (((1,), (0,)), ((), ()))
TN = (((0,), (0,)), ((), ()))


def dot(a, b, dims):
    return lax.dot_general(a, b, dims, preferred_element_type=F32)


def image_row(k, r):
    chunk, side = {0: (3, 0), 4: (3, 1), 1: (0, 0), 7: (0, 1), 2: (1, 0), 6: (1, 1), 3: (2, 0), 5: (2, 1)}[r]
    return chunk * 256 + side * 128 + k * 64


def text_row(h, p, q):
    if q == 0:
        at = h * 4 + p
    elif q == 2:
        at = 24 + h * 4 + p
    else:
        at = 8 + h * 8 + p * 2 + (q == 3)
    return at * HALF


def unit_rows(values):
    norm = jnp.sqrt(jnp.sum(values * values, axis=1, keepdims=True) + 1e-06)
    return values / norm, norm


def project_back(unit, norm, grads):
    inner = jnp.sum(unit * grads, axis=1, keepdims=True)
    return (grads - unit * inner) / norm


def pair_terms(scores, same, temperature, offset):
    logits = temperature * scores + offset
    e = jnp.exp(logits)
    u = 1.0 + e
    r = 1.0 / u
    slopes = jnp.where(same, -r, e * r)
    g = jnp.where(same, 1.0 / e, e)
    small = g * (1.0 - g * (0.5 - g * (1.0 / 3.0)))
    losses = jnp.where(g < 0.015625, small, jnp.log(1.0 + g))
    return losses, slopes


def kernel(pic, cap, warmth, bias, o_sum, o_pic, o_cap,
           img, txt, ih, il, th, tl, d_img, d_txt, s_ref, sh_ref, sl_ref, rid, cid, acc,
           got_s, got_z, got_t, sum_own, sum_z, sum_x, sum_y, sum_s,
           zs, zr, ss, sr, ts, tr, rzs, rzr, rss, rsr, rts, rtr, qs, qr):
    im = lax.axis_index("img")
    tx = lax.axis_index("txt")
    z, x = im // NX, im % NX
    y, c = tx // 2, tx % 2

    def at(dx=0, dy=0, dz=0, dc=0):
        return (((z + dz) % NZ) * NX + (x + dx) % NX, ((y + dy) % NY) * 2 + (c + dc) % 2)

    near = {"x+": at(dx=1), "x-": at(dx=3), "y+": at(dy=1), "y-": at(dy=3), "z+": at(dz=1), "z-": at(dz=7), "s": at(dc=1)}
    others = list(near.values()) + [at(dz=k) for k in (2, 3, 4, 5, 6)] + [at(dx=2), at(dy=2)]
    barrier = pltpu.get_barrier_semaphore()
    for other in others:
        pl.semaphore_signal(barrier, inc=1, device_id=other, device_id_type=MESH)

    pic_unit, pic_norm = unit_rows(pic[...])
    cap_unit, cap_norm = unit_rows(cap[...])
    own_i = image_row(0, 0)
    img[own_i:own_i + SHARD, :] = pic_unit
    for h in (0, 1):
        t0 = text_row(h, 0, 0)
        txt[t0:t0 + HALF, :] = cap_unit[h * HALF:(h + 1) * HALF, :]
    temperature = jnp.exp(warmth[0:1, 0:1])
    offset = bias[0:1, 0:1]

    for k in (0, 1):
        for r in range(NZ):
            block = (((z + NZ - r) % NZ) * NX + x) * (2 * NY) + y * 2 + (c + k) % 2
            base = image_row(k, r)
            rid[base:base + SHARD, :] = block * SHARD + lax.broadcasted_iota(jnp.int32, (SHARD, 128), 0)
    lane = lax.broadcasted_iota(jnp.int32, (8, 128), 1)
    for tile in range(ROWS // 128):
        ids = jnp.zeros((8, 128), jnp.int32)
        for h in (0, 1):
            for p in range(4):
                for q in range(4):
                    pos = text_row(h, p, q)
                    if pos // 128 == tile:
                        a, b = (p, q) if h == 0 else (q, p)
                        block = (((y + NY - b) % NY) * 2 + c) * (NX * NZ) + z * NX + (x + NX - a) % NX
                        off = pos % 128
                        inside = (lane >= off) & (lane < off + HALF)
                        ids = jnp.where(inside, block * SHARD + h * HALF + lane - off, ids)
        cid[:, tile * 128:(tile + 1) * 128] = ids

    pl.semaphore_wait(barrier, len(others))

    def remote(src, dst, s, r, dev):
        return pltpu.make_async_remote_copy(src_ref=src, dst_ref=dst, send_sem=s, recv_sem=r, device_id=dev, device_id_type=MESH)

    pending = []

    def go(copy):
        copy.start()
        pending.append(copy)

    def z_copy(s, d):
        src, dst = ((s - 1), s) if d == 0 else ((9 - s) % 8, 8 - s)
        off, n = (0, SHARD) if s < 4 else ((0, HALF) if d == 0 else (HALF, HALF))
        return remote(img.at[pl.ds(image_row(0, src) + off, n)], img.at[pl.ds(image_row(0, dst) + off, n)],
                      zs.at[s - 1, d], zr.at[s - 1, d], near["z+" if d == 0 else "z-"])

    def s_copy(r):
        return remote(img.at[pl.ds(image_row(0, r), SHARD)], img.at[pl.ds(image_row(1, r), SHARD)], ss.at[r], sr.at[r], near["s"])

    def t_index(h, phase, p, s, d):
        return h * 20 + (0 if phase == 0 else 4 + p * 4) + (s - 1) * 2 + d

    def t_copy(h, phase, p, s, d):
        src, dst = (s - 1, s) if d == 0 else ((5 - s) % 4, 4 - s)
        off, n = (0, HALF) if s < 2 else ((0, QUARTER) if d == 0 else (QUARTER, QUARTER))
        a, b = (text_row(h, src, 0), text_row(h, dst, 0)) if phase == 0 else (text_row(h, p, src), text_row(h, p, dst))
        i = t_index(h, phase, p, s, d)
        axis = ("xy", "yx")[h][phase]
        return remote(txt.at[pl.ds(a + off, n)], txt.at[pl.ds(b + off, n)], ts.at[i], tr.at[i], near[axis + ("+" if d == 0 else "-")])

    keys = [(h, 0, 0, s, d) for h in (0, 1) for s in (1, 2) for d in (0, 1)]
    keys += [(h, 1, p, s, d) for h in (0, 1) for p in range(4) for s in (1, 2) for d in (0, 1)]
    T = {k: t_copy(*k) for k in keys}
    Z = {(s, d): z_copy(s, d) for s in range(1, 5) for d in (0, 1)}
    S = {r: s_copy(r) for r in range(NZ)}
    HD = [(h, d) for d in (0, 1) for h in (0, 1)]

    for d in (0, 1):
        go(Z[1, d])
    for h, d in HD:
        go(T[h, 0, 0, 1, d])
    for h, d in HD:
        go(T[h, 1, 0, 1, d])
    go(S[0])
    for h, d in HD:
        T[h, 0, 0, 1, d].wait_recv()
        go(T[h, 0, 0, 2, d])
    for d in (0, 1):
        for h in (0, 1):
            for e in (0, 1):
                go(T[h, 1, 1 if d == 0 else 3, 1, e])
    for d in (0, 1):
        Z[1, d].wait_recv()
        go(Z[2, d])
    go(S[1])
    go(S[7])
    for h, d in HD:
        T[h, 0, 0, 2, d].wait_recv()
    for h in (0, 1):
        for e in (0, 1):
            go(T[h, 1, 2, 1, e])
    for h, d in HD:
        T[h, 1, 0, 1, d].wait_recv()
        go(T[h, 1, 0, 2, d])
    for d in (0, 1):
        Z[2, d].wait_recv()
        go(Z[3, d])
    go(S[2])
    go(S[6])
    for p in (1, 3):
        for h, d in HD:
            T[h, 1, p, 1, d].wait_recv()
            go(T[h, 1, p, 2, d])
    for d in (0, 1):
        Z[3, d].wait_recv()
        go(Z[4, d])
    go(S[3])
    go(S[5])
    for h, d in HD:
        T[h, 1, 2, 1, d].wait_recv()
        go(T[h, 1, 2, 2, d])
    for p in (0, 1, 3, 2):
        for h, d in HD:
            T[h, 1, p, 2, d].wait_recv()
    for d in (0, 1):
        Z[4, d].wait_recv()
    go(S[4])
    for r in range(NZ):
        S[r].wait_recv()
    for copy in pending:
        copy.wait_send()
    pending.clear()

    def split(i, _):
        rows = pl.ds(pl.multiple_of(i * 32, 32), 32)
        for src, hi, lo in ((img, ih, il), (txt, th, tl)):
            v = src[rows, :]
            top = v.astype(BF16)
            hi[rows, :] = top
            lo[rows, :] = (v - top.astype(F32)).astype(BF16)
        return 0

    lax.fori_loop(0, ROWS // 32, split, 0)
    d_txt[...] = jnp.zeros_like(d_txt)
    d_img[...] = jnp.zeros_like(d_img)
    acc[...] = jnp.zeros_like(acc)

    def tile(n, _):
        i, t = n // (ROWS // TT), n % (ROWS // TT)
        ri = pl.ds(pl.multiple_of(i * TI, TI), TI)
        rt = pl.ds(pl.multiple_of(t * TT, TT), TT)
        i_hi, i_lo, t_hi, t_lo = ih[ri, :], il[ri, :], th[rt, :], tl[rt, :]
        s_ref[...] = dot(jnp.concatenate([i_hi, i_lo, i_hi], 1), jnp.concatenate([t_hi, t_hi, t_lo], 1), NT)
        for b in range(TI // 32):
            scores = s_ref[b * 32:(b + 1) * 32, :]
            row = rid[pl.ds(pl.multiple_of(i * TI + b * 32, 32), 32), :]
            row = jnp.concatenate([row] * (TT // 128), 1)
            col = cid[:, rt]
            same = row == jnp.concatenate([col] * 4, 0)
            losses, slopes = pair_terms(scores, same, temperature, offset)
            for n_acc, v in enumerate((losses, slopes * scores, slopes)):
                acc[n_acc] += v[0:8] + v[8:16] + v[16:24] + v[24:32]
            hi = slopes.astype(BF16)
            sh_ref[b * 32:(b + 1) * 32, :] = hi
            sl_ref[b * 32:(b + 1) * 32, :] = (slopes - hi.astype(F32)).astype(BF16)
        sh, sl = sh_ref[...], sl_ref[...]
        d_img[ri, :] += dot(jnp.concatenate([sh, sl, sh], 1), jnp.concatenate([t_hi, t_hi, t_lo], 0), NN)
        d_txt[rt, :] += dot(jnp.concatenate([sh, sl, sh], 0), jnp.concatenate([i_hi, i_hi, i_lo], 0), TN)
        return 0

    lax.fori_loop(0, (ROWS // TI) * (ROWS // TT), tile, 0)

    for n_acc in range(3):
        v = acc[n_acc]
        v = v[:, 0:128] + v[:, 128:256] + v[:, 256:384] + v[:, 384:512]
        sum_own[0, n_acc:n_acc + 1, :] = jnp.sum(v, axis=0, keepdims=True)
    sum_own[0, 3:8, :] = jnp.zeros((5, 128), F32)

    def fan(stage, buf, size, base, where):
        copies = [remote(sum_own.at[stage], buf.at[k - 1], qs.at[base + k - 1], qr.at[base + k - 1], where(k)) for k in range(1, size)]
        for copy in copies:
            go(copy)
        return copies

    def fold(stage, buf, copies):
        total = sum_own[stage]
        for k, copy in enumerate(copies):
            copy.wait_recv()
            total = total + buf[k]
        sum_own[stage + 1] = total

    def rs_copy(r):
        return remote(d_img.at[pl.ds(image_row(1, r), SHARD)], got_s.at[r], rss.at[r], rsr.at[r], near["s"])

    def rz_copy(s, d):
        r = s if d == 0 else 8 - s
        off, n = (0, SHARD) if s < 4 else ((0, HALF) if d == 0 else (HALF, HALF))
        return remote(d_img.at[pl.ds(image_row(0, r) + off, n)], got_z.at[s - 1, d, pl.ds(0, n)],
                      rzs.at[s - 1, d], rzr.at[s - 1, d], near["z-" if d == 0 else "z+"])

    def rt_copy(h, phase, p, s, d):
        q = s if d == 0 else 4 - s
        off, n = (0, HALF) if s < 2 else ((0, QUARTER) if d == 0 else (QUARTER, QUARTER))
        a = text_row(h, q, 0) if phase == 0 else text_row(h, p, q)
        i = t_index(h, phase, p, s, d)
        axis = ("xy", "yx")[h][phase]
        return remote(d_txt.at[pl.ds(a + off, n)], got_t.at[i, pl.ds(0, n)], rts.at[i], rtr.at[i], near[axis + ("-" if d == 0 else "+")])

    RT = {k: rt_copy(*k) for k in keys}
    RZ = {(s, d): rz_copy(s, d) for s in range(1, 5) for d in (0, 1)}
    RS = {r: rs_copy(r) for r in range(NZ)}

    def add_t(h, phase, p, s, d):
        RT[h, phase, p, s, d].wait_recv()
        q = s - 1 if d == 0 else (5 - s) % 4
        off, n = (0, HALF) if s < 2 else ((0, QUARTER) if d == 0 else (QUARTER, QUARTER))
        a = (text_row(h, q, 0) if phase == 0 else text_row(h, p, q)) + off
        d_txt[a:a + n, :] += got_t[t_index(h, phase, p, s, d), 0:n, :]

    def add_z(s, d):
        RZ[s, d].wait_recv()
        r = s - 1 if d == 0 else (9 - s) % 8
        off, n = (0, SHARD) if s < 4 else ((0, HALF) if d == 0 else (HALF, HALF))
        a = image_row(0, r) + off
        d_img[a:a + n, :] += got_z[s - 1, d, 0:n, :]

    def add_s(r):
        RS[r].wait_recv()
        a = image_row(0, r)
        d_img[a:a + SHARD, :] += got_s[r]

    for r in (4, 3, 5, 2, 6, 1, 7, 0):
        go(RS[r])
    for p in (2, 1, 3, 0):
        for h, d in HD:
            go(RT[h, 1, p, 2, d])
    add_s(4)
    for d in (0, 1):
        go(RZ[4, d])
    z_sums = fan(0, sum_z, NZ, 0, lambda k: at(dz=k))
    for r in (3, 5, 2, 6, 1, 7, 0):
        add_s(r)
    for p in (2, 1, 3):
        for h, d in HD:
            add_t(h, 1, p, 2, d)
            go(RT[h, 1, p, 1, d])
        if p == 2:
            for d in (0, 1):
                add_z(4, d)
                go(RZ[3, d])
            fold(0, sum_z, z_sums)
            x_sums = fan(1, sum_x, NX, 7, lambda k: at(dx=k))
    for h, d in HD:
        add_t(h, 1, 0, 2, d)
        go(RT[h, 1, 0, 1, d])
    for d in (0, 1):
        add_z(3, d)
        go(RZ[2, d])
    fold(1, sum_x, x_sums)
    y_sums = fan(2, sum_y, NY, 10, lambda k: at(dy=k))
    for h, d in HD:
        add_t(h, 1, 2, 1, d)
    for h, d in HD:
        go(RT[h, 0, 0, 2, d])
    for d in (0, 1):
        add_z(2, d)
        go(RZ[1, d])
    fold(2, sum_y, y_sums)
    s_sums = fan(3, sum_s, 2, 13, lambda k: at(dc=1))
    for p in (1, 3):
        for h, d in HD:
            add_t(h, 1, p, 1, d)
    for h, d in HD:
        add_t(h, 0, 0, 2, d)
        go(RT[h, 0, 0, 1, d])
    for h, d in HD:
        add_t(h, 1, 0, 1, d)
    for d in (0, 1):
        add_z(1, d)
    o_pic[...] = project_back(pic_unit, pic_norm, temperature * d_img[own_i:own_i + SHARD, :])
    fold(3, sum_s, s_sums)
    totals = jnp.sum(sum_own[4], axis=1, keepdims=True) * (1.0 / 16384.0)
    kind = lax.broadcasted_iota(jnp.int32, (8, 1), 0)
    o_sum[...] = jnp.broadcast_to(jnp.where(kind == 1, temperature * totals, totals), (8, 128))
    for h, d in HD:
        add_t(h, 0, 0, 1, d)
    grads = jnp.concatenate([d_txt[text_row(h, 0, 0):text_row(h, 0, 0) + HALF, :] for h in (0, 1)], 0)
    o_cap[...] = project_back(cap_unit, cap_norm, temperature * grads)
    for copy in pending:
        copy.wait_send()


def body(picture_vectors, caption_vectors, warmth_exponent, offset_weight):
    vmem = pl.BlockSpec(memory_space=pltpu.VMEM)
    dma = pltpu.SemaphoreType.DMA
    big, split = pltpu.VMEM((ROWS, D), F32), pltpu.VMEM((ROWS, D), BF16)
    sums, picture_derivative, caption_derivative = pl.pallas_call(
        kernel,
        out_shape=[jax.ShapeDtypeStruct((8, 128), F32), jax.ShapeDtypeStruct((SHARD, D), F32), jax.ShapeDtypeStruct((SHARD, D), F32)],
        in_specs=[vmem] * 4,
        out_specs=[vmem] * 3,
        scratch_shapes=[
            big, big, split, split, split, split, big, big,
            pltpu.VMEM((TI, TT), F32), pltpu.VMEM((TI, TT), BF16), pltpu.VMEM((TI, TT), BF16),
            pltpu.VMEM((ROWS, 128), jnp.int32), pltpu.VMEM((8, ROWS), jnp.int32), pltpu.VMEM((3, 8, TT), F32),
            pltpu.VMEM((NZ, SHARD, D), F32), pltpu.VMEM((4, 2, SHARD, D), F32), pltpu.VMEM((40, HALF, D), F32),
            pltpu.VMEM((5, 8, 128), F32), pltpu.VMEM((7, 8, 128), F32), pltpu.VMEM((3, 8, 128), F32),
            pltpu.VMEM((3, 8, 128), F32), pltpu.VMEM((1, 8, 128), F32),
            dma((4, 2)), dma((4, 2)), dma((NZ,)), dma((NZ,)), dma((40,)), dma((40,)),
            dma((4, 2)), dma((4, 2)), dma((NZ,)), dma((NZ,)), dma((40,)), dma((40,)), dma((14,)), dma((14,)),
        ],
        compiler_params=pltpu.CompilerParams(collective_id=0, has_side_effects=True, vmem_limit_bytes=60 * 2**20),
    )(
        picture_vectors,
        caption_vectors,
        jnp.broadcast_to(warmth_exponent.reshape(1, 1), (8, 128)),
        jnp.broadcast_to(offset_weight.reshape(1, 1), (8, 128)),
    )
    return sums[0, 0:1], picture_derivative, caption_derivative, sums[1, 0:1], sums[2, 0:1]


def solution(mesh):
    in_specs = (P(("img", "txt"), None), P(("txt", "img"), None), P(), P())
    out_specs = (P(), P(("img", "txt"), None), P(("txt", "img"), None), P(), P())
    return jax.shard_map(body, mesh=mesh, in_specs=in_specs, out_specs=out_specs, check_vma=False)
```

time: 489 us -> 109 us (0.22); the launches traced: 483 us -> 108 us
  waiting for transfers between devices: 297 us -> 0 us
  Pallas kernels: 0 us -> 101 us
  blocking collectives: 76.2 us -> 0 us
  matrix products: 66.5 us -> 0 us
  other arithmetic: 18.8 us -> 0 us
  between operations: 20.7 us -> 1.93 us
    reduce_scatter x2 -> x0, waiting for transfers between devices: 161 us -> none  [the longest x1 161 us: body(): lax.psum_scatter(warmth_multiplier * jnp.dot(piece.T, image_unit, precisi...]
    all_gather x2 -> x0, waiting for transfers between devices: 134 us -> none  [the longest x1 102 us: body(): text_block = lax.all_gather(caption_vectors, 'img', axis=0, tiled=True)]
    pallas_call x0 -> x1, Pallas kernels: none -> 101 us  [body(): pl.pallas_call(kernel, out_shape=[jax.ShapeDtypeStruct((8, 128), F32), ja...]
    psum x1 -> x0, blocking collectives: 76.2 us -> none  [body(): penalty_accrued = lax.psum(local_loss, ('img', 'txt'))]
    dot_general x3 -> x0, matrix products: 66.5 us -> none  [the longest x1 24.8 us: body(): jnp.dot(image_unit, caption_unitlength.T, precision=full_accuracy_mode, p...]
    div x4 -> x0, other arithmetic: 10.1 us -> none  [the longest x2 6.39 us: unit_rows(): return (values / row_norm, row_norm)]
    reduce_sum x4 -> x0, other arithmetic: 8.68 us -> none  [the longest x2 6.41 us: unit_rows(): row_norm = jnp.sqrt(jnp.sum(values * values, axis=1, keepdims=True) + 1e-06)]
  transfers between devices with their start and end apart: 4 -> 0, of which waited for: 3 -> 0; matrix products, arithmetic and copies ran while one was open for 6% -> 0% of each run, Pallas kernels for 0% -> 0%
where the time goes in v1:
time: 109 us; the launch traced here: 108 us
  Pallas kernels  101 us (93%)
  local copies, waits for them, and re-layouts  4.95 us (5%)
  between operations  1.93 us (2%)
    pallas_call x1, Pallas kernels, body(): pl.pallas_call(kernel, out_shape=[jax.ShapeDtypeStruct((8, 128), F32), ja...  101 us
    unnamed x4, local copies, waits for them, and re-layouts  2.46 us

profile of v1, /device:TPU:1, one launch (start us, length us, event | category | flops | bytes accessed | tf_op | source)
XLA Modules:
  0.0 108.3 jit_solution(16919592429825380253)
XLA Ops:
  1.9 0.6 broadcast_in_dim.15.warmth
  2.5 0.6 broadcast_in_dim.17.bias
  3.1 101.4 %shard_map.83 = (f32[8,128]{1,0:T(8,128)}, f32[64,1152]{1,0:T(8,128)}, f32[64,1152]{1,0:T(8,128)}) custom-call(f32[64,1152]{1,0:T(8,128)} %pic.1, f32[64,1152]{1,0:T(8,128)} %cap.1, f32[8,128]{1,0:T(8,128)} %broadcast_in_dim.15.warmth, f32[8,128]{1,0:T(8,128)} %broadcast_in_dim.17.bias), custom_call_target="tpu_custom_call" | custom-call | tf_op jit(solution)/shard_map/pallas_call | solution.py:367
  104.6 1.3 %fusion = (f32[1,1]{1,0:T(1,128)}, f32[1,1]{1,0:T(1,128)}, f32[1,1]{1,0:T(1,128)}) fusion(f32[8,128]{1,0:T(8,128)} %get-tuple-element.8), kind=kLoop, calls=%fused_computation | loop fusion | bytes 24 | tf_op jit(solution)/shard_map/slice | solution.py:389
  105.9 0.0 copy-start
  105.9 1.7 %copy.13 = f32[64,1152]{1,0:T(8,128)} copy(f32[64,1152]{1,0:T(8,128)} %get-tuple-element.20) | data formatting | bytes 589824
  107.6 0.0 copy-done
  107.6 0.7 copy.14
Async XLA Ops:
  105.9 1.7 %copy-start = (f32[64,1152]{1,0:T(8,128)S(1)}, f32[64,1152]{1,0:T(8,128)}, u32[]{:S(2)}) copy-start(f32[64,1152]{1,0:T(8,128)} %get-tuple-element.21) | copy-start | bytes 884740

commit v2 on v0

v2 whole, which is shorter than its diff:
```python
import functools

import jax
import jax.numpy as jnp
from jax import lax
from jax.experimental import pallas as pl
from jax.experimental.pallas import tpu as pltpu
from jax.sharding import PartitionSpec as P

MESH = pl.DeviceIdType.MESH
F32, BF16, F8 = jnp.float32, jnp.bfloat16, jnp.float8_e4m3fn
UP = 4096.0
NX, NY, NZ = 4, 4, 8
SHARD, HALF, QUARTER, D = 64, 32, 16, 1152
ROWS = 1024
SHARE = {0: 0, 1: 1, 7: 1, 2: 2, 6: 2, 3: 3, 5: 3, 4: 3}
BACK = {4: 0, 3: 1, 5: 1, 2: 2, 6: 2, 1: 2, 7: 2, 0: 2}
NT = (((1,), (1,)), ((), ()))
NN = (((1,), (0,)), ((), ()))
TN = (((0,), (0,)), ((), ()))


def dot(a, b, dims):
    return lax.dot_general(a, b, dims, preferred_element_type=F32)


def image_row(k, r):
    return {0: 0, 1: 128, 7: 256, 2: 384, 6: 512, 3: 640, 5: 768, 4: 896}[r] + k * SHARD


def text_row(h, p, q):
    if q == 0:
        at = h * 4 + p
    elif q == 2:
        at = 24 + h * 4 + p
    else:
        at = 8 + h * 8 + p * 2 + (q == 3)
    return at * HALF


def unit_rows(values):
    norm = jnp.sqrt(jnp.sum(values * values, axis=1, keepdims=True) + 1e-06)
    return values / norm, norm


def project_back(unit, norm, grads):
    inner = jnp.sum(unit * grads, axis=1, keepdims=True)
    return (grads - unit * inner) / norm


def pair_terms(scores, same, temperature, offset):
    logits = temperature * scores + offset
    e = jnp.exp(logits)
    u = 1.0 + e
    r = 1.0 / u
    slopes = jnp.where(same, -r, e * r)
    g = jnp.where(same, 1.0 / e, e)
    small = g * (1.0 - g * (0.5 - g * (1.0 / 3.0)))
    losses = jnp.where(g < 0.015625, small, jnp.log(1.0 + g))
    return losses, slopes


def kernel(pic, cap, warmth, bias, o_sum, o_pic, o_cap,
           img, txt, ih, il, th, tl, ih8, il8, th8, tl8, d_img, d_txt, s_ref, sh_ref, sh8_ref, sl8_ref, rid, cid, acc,
           got_s, got_z, got_t, sum_own, sum_got, zr, sr, tr, rzr, rsr, rtr, qr, sent):
    im = lax.axis_index("img")
    tx = lax.axis_index("txt")
    z, x = im // NX, im % NX
    y, c = tx // 2, tx % 2

    def at(dx=0, dy=0, dz=0, dc=0):
        return (((z + dz) % NZ) * NX + (x + dx) % NX, ((y + dy) % NY) * 2 + (c + dc) % 2)

    near = {"x+": at(dx=1), "x-": at(dx=3), "y+": at(dy=1), "y-": at(dy=3), "z+": at(dz=1), "z-": at(dz=7), "s": at(dc=1)}
    others = list(near.values()) + [at(dz=k) for k in (2, 3, 4, 5, 6)] + [at(dx=2), at(dy=2)]
    barrier = pltpu.get_barrier_semaphore()
    for other in others:
        pl.semaphore_signal(barrier, inc=1, device_id=other, device_id_type=MESH)

    pic_unit, pic_norm = unit_rows(pic[...])
    cap_unit, cap_norm = unit_rows(cap[...])
    own_i = image_row(0, 0)
    img[own_i:own_i + SHARD, :] = pic_unit
    for h in (0, 1):
        t0 = text_row(h, 0, 0)
        txt[t0:t0 + HALF, :] = cap_unit[h * HALF:(h + 1) * HALF, :]
    temperature = jnp.exp(jnp.full((1, 1), warmth[0], F32))
    offset = jnp.full((1, 1), bias[0], F32)
    warm_down = temperature * (1.0 / (UP * UP))

    pl.semaphore_wait(barrier, len(others))

    def remote(src, dst, s, r, dev):
        return pltpu.make_async_remote_copy(src_ref=src, dst_ref=dst, send_sem=s, recv_sem=r, device_id=dev, device_id_type=MESH)

    def landed(rows, sem):
        pltpu.make_async_copy(d_img.at[pl.ds(0, rows)], d_img.at[pl.ds(0, rows)], sem).wait()

    def go(copy):
        copy.start()

    def z_group(s, d, h):
        return (s - 1) * 2 + ((h if d == 0 else 1 - h) if s < 4 else 0)

    def t_group(phase, p, s):
        return (0 if phase == 0 else 2 + 2 * p) + s - 1

    def z_copy(s, d, h):
        src, dst = ((s - 1), s) if d == 0 else ((9 - s) % 8, 8 - s)
        return remote(img.at[pl.ds(image_row(0, src) + h * HALF, HALF)], img.at[pl.ds(image_row(0, dst) + h * HALF, HALF)],
                      sent.at[0], zr.at[z_group(s, d, h)], near["z+" if d == 0 else "z-"])

    def s_copy(r):
        return remote(img.at[pl.ds(image_row(0, r), SHARD)], img.at[pl.ds(image_row(1, r), SHARD)], sent.at[1], sr.at[SHARE[r]], near["s"])

    def t_index(h, phase, p, s, d):
        return h * 20 + (0 if phase == 0 else 4 + p * 4) + (s - 1) * 2 + d

    def t_copy(h, phase, p, s, d):
        src, dst = (s - 1, s) if d == 0 else ((5 - s) % 4, 4 - s)
        off, n = (0, HALF) if s < 2 else ((0, QUARTER) if d == 0 else (QUARTER, QUARTER))
        a, b = (text_row(h, src, 0), text_row(h, dst, 0)) if phase == 0 else (text_row(h, p, src), text_row(h, p, dst))
        axis = ("xy", "yx")[h][phase]
        return remote(txt.at[pl.ds(a + off, n)], txt.at[pl.ds(b + off, n)], sent.at[2], tr.at[t_group(phase, p, s)], near[axis + ("+" if d == 0 else "-")])

    keys = [(h, 0, 0, s, d) for h in (0, 1) for s in (1, 2) for d in (0, 1)]
    keys += [(h, 1, p, s, d) for h in (0, 1) for p in range(4) for s in (1, 2) for d in (0, 1)]
    z_keys = [(s, d, h) for s in (1, 2, 3) for d in (0, 1) for h in (0, 1)] + [(4, 0, 0), (4, 1, 1)]
    T = {k: t_copy(*k) for k in keys}
    Z = {k: z_copy(*k) for k in z_keys}
    S = {r: s_copy(r) for r in range(NZ)}
    HD = [(h, d) for d in (0, 1) for h in (0, 1)]

    def pass_z(s, n):
        landed(2 * HALF, zr.at[z_group(s, 0, n)])
        for d in (0, 1):
            h = n if d == 0 else 1 - n
            if (s + 1, d, h) in Z:
                go(Z[s + 1, d, h])

    def pass_t(phase, p, s):
        landed(4 * HALF if s == 1 else 4 * QUARTER, tr.at[t_group(phase, p, s)])
        for h, d in HD:
            if s == 1:
                go(T[h, phase, p, 2, d])

    def share(*rs):
        for r in rs:
            go(S[r])

    def split(src, hi, lo, hi8, lo8, first, last):
        def step(i, _):
            rows = pl.ds(pl.multiple_of(first + i * 32, 32), 32)
            v = src[rows, :] * UP
            top = v.astype(BF16)
            rest = v - top.astype(F32)
            hi[rows, :] = top
            lo[rows, :] = rest.astype(BF16)
            hi8[rows, :] = (v * 0.0625).astype(F8)
            lo8[rows, :] = (rest * 16.0).astype(F8)
            return 0

        lax.fori_loop(0, (last - first) // 32, step, 0)

    def split_i(first, last):
        split(img, ih, il, ih8, il8, first, last)

    def split_t(first, last):
        split(txt, th, tl, th8, tl8, first, last)

    def block(i0, i1, t0, t1, first_i, first_t):
        ri, rt = slice(i0, i1), slice(t0, t1)
        ni, nt = i1 - i0, t1 - t0
        i_hi, i_lo, t_hi, t_lo = ih[ri, :], il[ri, :], th[rt, :], tl[rt, :]
        s_ref[ri, rt] = dot(jnp.concatenate([i_hi, i_lo, i_hi], 1), jnp.concatenate([t_hi, t_hi, t_lo], 1), NT)
        n = max(8192 // nt // 32, 1) * 32
        sums = [jnp.zeros((8, nt), F32)] * 3
        for b in range(i0, i1, n):
            rows = slice(b, b + n)
            scores = s_ref[rows, rt]
            row = jnp.concatenate([rid[rows, :]] * (nt // 128), 1)
            same = row == jnp.concatenate([cid[:, rt]] * (n // 8), 0)
            losses, slopes = pair_terms(scores, same, warm_down, offset)
            sums = [a + jnp.sum(v.reshape(n // 8, 8, nt), axis=0) for a, v in zip(sums, (losses, slopes * scores, slopes))]
            slopes = slopes * UP
            hi = slopes.astype(BF16)
            sh_ref[rows, rt] = hi
            sh8_ref[rows, rt] = (slopes * 0.0625).astype(F8)
            sl8_ref[rows, rt] = ((slopes - hi.astype(F32)) * 16.0).astype(F8)
        for k, v in enumerate(sums):
            acc[k] += sum(v[:, q:q + 128] for q in range(0, nt, 128))
        sh, sh8, sl8 = sh_ref[ri, rt], sh8_ref[ri, rt], sl8_ref[ri, rt]
        g = dot(sh, t_hi, NN) + dot(jnp.concatenate([sl8, sh8], 1), jnp.concatenate([th8[rt, :], tl8[rt, :]], 0), NN)
        d_img[ri, :] = g if first_i else d_img[ri, :] + g
        g = dot(sh, i_hi, TN) + dot(jnp.concatenate([sl8, sh8], 0), jnp.concatenate([ih8[ri, :], il8[ri, :]], 0), TN)
        d_txt[rt, :] = g if first_t else d_txt[rt, :] + g

    for n in (0, 1):
        for d in (0, 1):
            go(Z[1, d, n if d == 0 else 1 - n])
    for h, d in HD:
        go(T[h, 0, 0, 1, d])
    for h, d in HD:
        go(T[h, 1, 0, 1, d])
    share(0)

    for k in (0, 1):
        for r in range(NZ):
            number = (((z + NZ - r) % NZ) * NX + x) * (2 * NY) + y * 2 + (c + k) % 2
            base = image_row(k, r)
            rid[base:base + SHARD, :] = number * SHARD + lax.broadcasted_iota(jnp.int32, (SHARD, 128), 0)
    lane = lax.broadcasted_iota(jnp.int32, (8, 128), 1)
    for part in range(ROWS // 128):
        ids = jnp.zeros((8, 128), jnp.int32)
        for h in (0, 1):
            for p in range(4):
                for q in range(4):
                    pos = text_row(h, p, q)
                    if pos // 128 == part:
                        a, b = (p, q) if h == 0 else (q, p)
                        number = (((y + NY - b) % NY) * 2 + c) * (NX * NZ) + z * NX + (x + NX - a) % NX
                        off = pos % 128
                        inside = (lane >= off) & (lane < off + HALF)
                        ids = jnp.where(inside, number * SHARD + h * HALF + lane - off, ids)
        cid[:, part * 128:(part + 1) * 128] = ids
    acc[...] = jnp.zeros_like(acc)

    pass_t(0, 0, 1)
    for p in (1, 3):
        for h in (0, 1):
            for d in (0, 1):
                go(T[h, 1, p, 1, d])
    pass_z(1, 0)
    landed(SHARD, sr.at[0])
    split_i(0, 128)
    pass_z(1, 1)
    share(1, 7)
    pass_t(0, 0, 2)
    for h in (0, 1):
        for d in (0, 1):
            go(T[h, 1, 2, 1, d])
    split_t(0, 256)
    pass_z(2, 0)
    landed(2 * SHARD, sr.at[1])
    split_i(128, 384)
    block(0, 384, 0, 256, True, True)
    pass_t(1, 0, 1)
    pass_z(2, 1)
    share(2, 6)
    pass_t(1, 1, 1)
    landed(2 * SHARD, sr.at[2])
    split_i(384, 640)
    pass_t(1, 3, 1)
    pass_z(3, 0)
    block(384, 640, 0, 256, True, False)
    pass_t(1, 2, 1)
    split_t(256, 768)
    pass_z(3, 1)
    share(3, 5)
    block(0, 384, 256, 768, False, True)
    landed(2 * HALF, zr.at[6])
    share(4)
    block(384, 640, 256, 768, False, False)
    for p in (0, 1, 3, 2):
        pass_t(1, p, 2)
    split_t(768, 1024)
    landed(3 * SHARD, sr.at[3])
    split_i(640, 1024)
    for k, rows in enumerate((14 * HALF, NZ * SHARD, 15 * SHARD)):
        landed(rows, sent.at[k])

    def rs_copy(r):
        return remote(d_img.at[pl.ds(image_row(1, r), SHARD)], got_s.at[r], sent.at[1], rsr.at[BACK[r]], near["s"])

    def rz_copy(s, d, h):
        r = s if d == 0 else 8 - s
        return remote(d_img.at[pl.ds(image_row(0, r) + h * HALF, HALF)], got_z.at[s - 1, d, pl.ds(h * HALF, HALF)],
                      sent.at[0], rzr.at[z_group(s, 1 - d, h)], near["z-" if d == 0 else "z+"])

    def rt_copy(h, phase, p, s, d):
        q = s if d == 0 else 4 - s
        off, n = (0, HALF) if s < 2 else ((0, QUARTER) if d == 0 else (QUARTER, QUARTER))
        a = text_row(h, q, 0) if phase == 0 else text_row(h, p, q)
        i = t_index(h, phase, p, s, d)
        axis = ("xy", "yx")[h][phase]
        return remote(d_txt.at[pl.ds(a + off, n)], got_t.at[i, pl.ds(0, n)], sent.at[2], rtr.at[t_group(phase, p, s)], near[axis + ("-" if d == 0 else "+")])

    RT = {k: rt_copy(*k) for k in keys}
    RZ = {k: rz_copy(*k) for k in z_keys}
    RS = {r: rs_copy(r) for r in range(NZ)}

    def add_t(h, phase, p, s, d):
        q = s - 1 if d == 0 else (5 - s) % 4
        off, n = (0, HALF) if s < 2 else ((0, QUARTER) if d == 0 else (QUARTER, QUARTER))
        a = (text_row(h, q, 0) if phase == 0 else text_row(h, p, q)) + off
        d_txt[a:a + n, :] += got_t[t_index(h, phase, p, s, d), 0:n, :]

    def add_z(s, d, h):
        r = s - 1 if d == 0 else (9 - s) % 8
        a = image_row(0, r) + h * HALF
        d_img[a:a + HALF, :] += got_z[s - 1, d, h * HALF:(h + 1) * HALF, :]

    def add_s(r):
        a = image_row(0, r)
        d_img[a:a + SHARD, :] += got_s[r]

    def back_t(phase, p, s, then=None):
        landed(4 * HALF if s == 1 else 4 * QUARTER, rtr.at[t_group(phase, p, s)])
        for h, d in HD:
            add_t(h, phase, p, s, d)
            if then is not None:
                go(RT[(h,) + then + (d,)])

    def back_z(s, n):
        landed(2 * HALF, rzr.at[z_group(s, 0, n)])
        for d in (0, 1):
            h = (1 - n if d == 0 else n) if s < 4 else d
            add_z(s, d, h)
            if s > 1:
                go(RZ[s - 1, d, h])

    STAGES = ((0, NZ, lambda k: at(dz=k)), (7, NX, lambda k: at(dx=k)), (10, NY, lambda k: at(dy=k)), (13, 2, lambda k: at(dc=k)))

    def fan(stage):
        base, size, where = STAGES[stage]
        for k in range(1, size):
            go(remote(sum_own.at[stage], sum_got.at[base + k - 1], sent.at[3], qr.at[stage], where(k)))

    def fold(stage):
        base, size, _ = STAGES[stage]
        got = sum_got.at[pl.ds(base, size - 1)]
        pltpu.make_async_copy(got, got, qr.at[stage]).wait()
        total = sum_own[stage]
        for k in range(base, base + size - 1):
            total = total + sum_got[k]
        sum_own[stage + 1] = total

    block(0, 512, 768, 1024, False, True)
    block(512, 640, 768, 1024, False, False)
    block(640, 1024, 768, 1024, True, False)
    for p in (2, 1, 3, 0):
        for h, d in HD:
            go(RT[h, 1, p, 2, d])
    block(896, 1024, 0, 768, False, False)
    go(RS[4])
    block(640, 896, 0, 256, False, False)
    landed(SHARD, rsr.at[0])
    add_s(4)
    for d in (0, 1):
        go(RZ[4, d, d])
    block(640, 896, 256, 768, False, False)
    for r in (3, 5, 2, 6, 1, 7, 0):
        go(RS[r])
    for k in range(3):
        sum_own[0, k:k + 1, :] = jnp.sum(acc[k], axis=0, keepdims=True)
    sum_own[0, 3:8, :] = jnp.zeros((5, 128), F32)
    fan(0)
    back_t(1, 2, 2, (1, 2, 1))
    landed(2 * SHARD, rsr.at[1])
    for r in (3, 5):
        add_s(r)
    for d in (0, 1):
        go(RZ[3, d, 1 - d])
    back_z(4, 0)
    for p in (1, 3, 0):
        back_t(1, p, 2, (1, p, 1))
    landed(5 * SHARD, rsr.at[2])
    for r in (2, 6, 1, 7, 0):
        add_s(r)
    fold(0)
    fan(1)
    back_z(3, 0)
    back_t(1, 2, 1)
    for h, d in HD:
        go(RT[h, 0, 0, 2, d])
    back_z(3, 1)
    fold(1)
    fan(2)
    back_t(1, 1, 1)
    back_z(2, 0)
    back_t(1, 3, 1)
    back_t(0, 0, 2, (0, 0, 1))
    back_z(2, 1)
    fold(2)
    fan(3)
    back_z(1, 0)
    back_t(1, 0, 1)
    back_z(1, 1)
    o_pic[...] = project_back(pic_unit, pic_norm, warm_down * d_img[own_i:own_i + SHARD, :])
    fold(3)
    totals = jnp.sum(sum_own[4], axis=1, keepdims=True) * (1.0 / 16384.0)
    kind = lax.broadcasted_iota(jnp.int32, (8, 1), 0)
    o_sum[...] = jnp.broadcast_to(jnp.where(kind == 1, warm_down * totals, totals), (8, 128))
    back_t(0, 0, 1)
    grads = jnp.concatenate([d_txt[text_row(h, 0, 0):text_row(h, 0, 0) + HALF, :] for h in (0, 1)], 0)
    o_cap[...] = project_back(cap_unit, cap_norm, warm_down * grads)
    for k, rows in enumerate((14 * HALF, NZ * SHARD, 15 * SHARD)):
        landed(rows, sent.at[k])
    pltpu.make_async_copy(sum_got, sum_got, sent.at[3]).wait()


def finish(sums, pic, cap, o_loss, o_pic, o_cap, o_warmth, o_bias):
    o_loss[...] = sums[0:1, 0:1]
    o_warmth[...] = sums[1:2, 0:1]
    o_bias[...] = sums[2:3, 0:1]
    o_pic[...] = pic[...]
    o_cap[...] = cap[...]


def body(picture_vectors, caption_vectors, warmth_exponent, offset_weight):
    vmem, smem = pl.BlockSpec(memory_space=pltpu.VMEM), pl.BlockSpec(memory_space=pltpu.SMEM)
    dma = pltpu.SemaphoreType.DMA
    big, split, eighth = pltpu.VMEM((ROWS, D), F32), pltpu.VMEM((ROWS, D), BF16), pltpu.VMEM((ROWS, D), F8)
    one, shard = jax.ShapeDtypeStruct((1, 1), F32), jax.ShapeDtypeStruct((SHARD, D), F32)
    results = pl.pallas_call(
        kernel,
        out_shape=[jax.ShapeDtypeStruct((8, 128), F32), shard, shard],
        in_specs=[vmem, vmem, smem, smem],
        out_specs=[vmem] * 3,
        scratch_shapes=[
            big, big, split, split, split, split, eighth, eighth, eighth, eighth, big, big,
            pltpu.VMEM((ROWS, ROWS), F32), pltpu.VMEM((ROWS, ROWS), BF16), pltpu.VMEM((ROWS, ROWS), F8), pltpu.VMEM((ROWS, ROWS), F8),
            pltpu.VMEM((ROWS, 128), jnp.int32), pltpu.VMEM((8, ROWS), jnp.int32), pltpu.VMEM((3, 8, 128), F32),
            pltpu.VMEM((NZ, SHARD, D), F32), pltpu.VMEM((4, 2, SHARD, D), F32), pltpu.VMEM((40, HALF, D), F32),
            pltpu.VMEM((5, 8, 128), F32), pltpu.VMEM((14, 8, 128), F32),
            dma((7,)), dma((4,)), dma((10,)), dma((7,)), dma((3,)), dma((10,)), dma((4,)), dma((4,)),
        ],
        compiler_params=pltpu.CompilerParams(collective_id=0, has_side_effects=True, vmem_limit_bytes=62 * 2**20),
    )(picture_vectors, caption_vectors, warmth_exponent, offset_weight)
    loss, picture_derivative, caption_derivative, warmth, bias = pl.pallas_call(
        finish, out_shape=[one, shard, shard, one, one], in_specs=[vmem] * 3, out_specs=[vmem] * 5
    )(*results)
    return loss.reshape(1), picture_derivative, caption_derivative, warmth.reshape(1), bias.reshape(1)


def solution(mesh):
    in_specs = (P(("img", "txt"), None), P(("txt", "img"), None), P(), P())
    out_specs = (P(), P(("img", "txt"), None), P(("txt", "img"), None), P(), P())
    return jax.shard_map(body, mesh=mesh, in_specs=in_specs, out_specs=out_specs, check_vma=False)
```

time: 489 us -> 90.8 us (0.19); the launches traced: 483 us -> 90.6 us
  waiting for transfers between devices: 297 us -> 0 us
  Pallas kernels: 0 us -> 88.7 us
  blocking collectives: 76.2 us -> 0 us
  matrix products: 66.5 us -> 0 us
  other arithmetic: 18.8 us -> 0 us
  between operations: 20.7 us -> 1.93 us
    reduce_scatter x2 -> x0, waiting for transfers between devices: 161 us -> none  [the longest x1 161 us: body(): lax.psum_scatter(warmth_multiplier * jnp.dot(piece.T, image_unit, precisi...]
    all_gather x2 -> x0, waiting for transfers between devices: 134 us -> none  [the longest x1 102 us: body(): text_block = lax.all_gather(caption_vectors, 'img', axis=0, tiled=True)]
    pallas_call x0 -> x2, Pallas kernels: none -> 88.7 us  [the longest x1 86.8 us: body(): pl.pallas_call(kernel, out_shape=[jax.ShapeDtypeStruct((8, 128), F32), sh...]
    psum x1 -> x0, blocking collectives: 76.2 us -> none  [body(): penalty_accrued = lax.psum(local_loss, ('img', 'txt'))]
    dot_general x3 -> x0, matrix products: 66.5 us -> none  [the longest x1 24.8 us: body(): jnp.dot(image_unit, caption_unitlength.T, precision=full_accuracy_mode, p...]
    div x4 -> x0, other arithmetic: 10.1 us -> none  [the longest x2 6.39 us: unit_rows(): return (values / row_norm, row_norm)]
    reduce_sum x4 -> x0, other arithmetic: 8.68 us -> none  [the longest x2 6.41 us: unit_rows(): row_norm = jnp.sqrt(jnp.sum(values * values, axis=1, keepdims=True) + 1e-06)]
  transfers between devices with their start and end apart: 4 -> 0, of which waited for: 3 -> 0; matrix products, arithmetic and copies ran while one was open for 6% -> 0% of each run, Pallas kernels for 0% -> 0%
where the time goes in v2:
time: 90.8 us; the launch traced here: 90.6 us
  Pallas kernels  88.7 us (98%)
  between operations  1.93 us (2%)
    pallas_call x1, Pallas kernels, body(): pl.pallas_call(kernel, out_shape=[jax.ShapeDtypeStruct((8, 128), F32), sh...  86.8 us
    pallas_call x1, Pallas kernels, body(): pl.pallas_call(finish, out_shape=[one, shard, shard, one, one], in_specs=...  1.9 us

profile of v2, /device:TPU:1, one launch (start us, length us, event | category | flops | bytes accessed | tf_op | source)
XLA Modules:
  0.0 90.6 jit_solution(393832662745920690)
XLA Ops:
  1.9 86.8 %shard_map.83 = (f32[8,128]{1,0:T(8,128)}, f32[64,1152]{1,0:T(8,128)}, f32[64,1152]{1,0:T(8,128)}) custom-call(f32[64,1152]{1,0:T(8,128)} %pic.1, f32[64,1152]{1,0:T(8,128)} %cap.1, f32[1]{0:T(128)S(6)} %copy.9.warmth, f32[1]{0:T(128)S(6)} %copy.10.bias), custom_call_target="tpu_custom_call" | custom-call | tf_op jit(solution)/shard_map/pallas_call | solution.py:415
  88.7 1.9 %shard_map.84 = (f32[1,1]{1,0:T(1,128)}, f32[64,1152]{1,0:T(8,128)}, f32[64,1152]{1,0:T(8,128)}, f32[1,1]{1,0:T(1,128)}, f32[1,1]{1,0:T(1,128)}) custom-call(f32[8,128]{1,0:T(8,128)} %get-tuple-element.13.sums, f32[64,1152]{1,0:T(8,128)} %get-tuple-element.14.pic, f32[64,1152]{1,0:T(8,128)} %get-tuple-element.15.cap), custom_call_target="tpu_custom_call" | custom-call | tf_op jit(solution)/shard_map/pallas_call | solution.py:430

commit v3 on v2

--- a/solution.py
+++ b/solution.py
@@ -34,7 +34,7 @@
     elif q == 2:
         at = 24 + h * 4 + p
     else:
-        at = 8 + h * 8 + p * 2 + (q == 3)
+        at = 8 + (0, 1, 3, 2)[p] * 4 + h * 2 + (q == 3)
     return at * HALF
 
 
@@ -61,7 +61,7 @@
 
 
 def kernel(pic, cap, warmth, bias, o_sum, o_pic, o_cap,
-           img, txt, ih, il, th, tl, ih8, il8, th8, tl8, d_img, d_txt, s_ref, sh_ref, sh8_ref, sl8_ref, rid, cid, acc,
+           img, txt, ih, il, th, tl, ih8, il8, th8, tl8, d_img, d_txt, s_ref, sh_ref, sh8_ref, sl8_ref, rid_i, cid_i, rid_t, cid_t, acc,
            got_s, got_z, got_t, sum_own, sum_got, zr, sr, tr, rzr, rsr, rtr, qr, sent):
     im = lax.axis_index("img")
     tx = lax.axis_index("txt")
@@ -168,32 +168,49 @@
     def split_t(first, last):
         split(txt, th, tl, th8, tl8, first, last)
 
-    def block(i0, i1, t0, t1, first_i, first_t):
-        ri, rt = slice(i0, i1), slice(t0, t1)
-        ni, nt = i1 - i0, t1 - t0
-        i_hi, i_lo, t_hi, t_lo = ih[ri, :], il[ri, :], th[rt, :], tl[rt, :]
-        s_ref[ri, rt] = dot(jnp.concatenate([i_hi, i_lo, i_hi], 1), jnp.concatenate([t_hi, t_hi, t_lo], 1), NT)
-        n = max(8192 // nt // 32, 1) * 32
-        sums = [jnp.zeros((8, nt), F32)] * 3
-        for b in range(i0, i1, n):
+    def block(i0, i1, t0, t1, first_i=False, first_t=False, across=False, flip=False, hooks=()):
+        hooks = dict(enumerate(hooks))
+        image = (ih, il, ih8, il8, d_img, rid_i, cid_i, slice(i0, i1), first_i)
+        text = (th, tl, th8, tl8, d_txt, rid_t, cid_t, slice(t0, t1), first_t)
+        (a_hi, a_lo, a_hi8, a_lo8, d_a, rid, _, ra, first_a) = text if across else image
+        (b_hi, b_lo, b_hi8, b_lo8, d_b, _, cid, rb, first_b) = image if across else text
+        na, nb = ra.stop - ra.start, rb.stop - rb.start
+        s_ref[ra, rb] = dot(jnp.concatenate([a_hi[ra, :], a_lo[ra, :], a_hi[ra, :]], 1),
+                            jnp.concatenate([b_hi[rb, :], b_hi[rb, :], b_lo[rb, :]], 1), NT)
+        if 0 in hooks:
+            hooks[0]()
+        n = max(16384 // nb // 32, 1) * 32
+        sums = [jnp.zeros((8, nb), F32)] * 3
+        for b in range(ra.start, ra.stop, n):
             rows = slice(b, b + n)
-            scores = s_ref[rows, rt]
-            row = jnp.concatenate([rid[rows, :]] * (nt // 128), 1)
-            same = row == jnp.concatenate([cid[:, rt]] * (n // 8), 0)
+            scores = s_ref[rows, rb]
+            row = jnp.concatenate([rid[rows, :]] * (nb // 128), 1)
+            same = row == jnp.concatenate([cid[:, rb]] * (n // 8), 0)
             losses, slopes = pair_terms(scores, same, warm_down, offset)
-            sums = [a + jnp.sum(v.reshape(n // 8, 8, nt), axis=0) for a, v in zip(sums, (losses, slopes * scores, slopes))]
+            sums = [u + jnp.sum(v.reshape(n // 8, 8, nb), axis=0) for u, v in zip(sums, (losses, slopes * scores, slopes))]
             slopes = slopes * UP
             hi = slopes.astype(BF16)
-            sh_ref[rows, rt] = hi
-            sh8_ref[rows, rt] = (slopes * 0.0625).astype(F8)
-            sl8_ref[rows, rt] = ((slopes - hi.astype(F32)) * 16.0).astype(F8)
+            sh_ref[rows, rb] = hi
+            sh8_ref[rows, rb] = (slopes * 0.0625).astype(F8)
+            sl8_ref[rows, rb] = ((slopes - hi.astype(F32)) * 16.0).astype(F8)
         for k, v in enumerate(sums):
-            acc[k] += sum(v[:, q:q + 128] for q in range(0, nt, 128))
-        sh, sh8, sl8 = sh_ref[ri, rt], sh8_ref[ri, rt], sl8_ref[ri, rt]
-        g = dot(sh, t_hi, NN) + dot(jnp.concatenate([sl8, sh8], 1), jnp.concatenate([th8[rt, :], tl8[rt, :]], 0), NN)
-        d_img[ri, :] = g if first_i else d_img[ri, :] + g
-        g = dot(sh, i_hi, TN) + dot(jnp.concatenate([sl8, sh8], 0), jnp.concatenate([ih8[ri, :], il8[ri, :]], 0), TN)
-        d_txt[rt, :] = g if first_t else d_txt[rt, :] + g
+            acc[k] += sum(v[:, q:q + 128] for q in range(0, nb, 128))
+        if 1 in hooks:
+            hooks[1]()
+        sh, sh8, sl8 = sh_ref[ra, rb], sh8_ref[ra, rb], sl8_ref[ra, rb]
+
+        def down():
+            g = dot(sh, b_hi[rb, :], NN) + dot(jnp.concatenate([sl8, sh8], 1), jnp.concatenate([b_hi8[rb, :], b_lo8[rb, :]], 0), NN)
+            d_a[ra, :] = g if first_a else d_a[ra, :] + g
+
+        def over():
+            g = dot(sh, a_hi[ra, :], TN) + dot(jnp.concatenate([sl8, sh8], 0), jnp.concatenate([a_hi8[ra, :], a_lo8[ra, :]], 0), TN)
+            d_b[rb, :] = g if first_b else d_b[rb, :] + g
+
+        (over if flip else down)()
+        if 2 in hooks:
+            hooks[2]()
+        (down if flip else over)()
 
     for n in (0, 1):
         for d in (0, 1):
@@ -204,12 +221,15 @@
         go(T[h, 1, 0, 1, d])
     share(0)
 
-    for k in (0, 1):
-        for r in range(NZ):
-            number = (((z + NZ - r) % NZ) * NX + x) * (2 * NY) + y * 2 + (c + k) % 2
-            base = image_row(k, r)
-            rid[base:base + SHARD, :] = number * SHARD + lax.broadcasted_iota(jnp.int32, (SHARD, 128), 0)
     lane = lax.broadcasted_iota(jnp.int32, (8, 128), 1)
+    for r in range(NZ):
+        number = (((z + NZ - r) % NZ) * NX + x) * (2 * NY) + y * 2
+        base = image_row(0, r)
+        for k in (0, 1):
+            rows = lax.broadcasted_iota(jnp.int32, (SHARD, 128), 0)
+            rid_i[base + k * SHARD:base + (k + 1) * SHARD, :] = (number + (c + k) % 2) * SHARD + rows
+        own, other = (number + c) * SHARD + lane, (number + (c + 1) % 2) * SHARD + lane - SHARD
+        cid_i[:, base:base + 128] = jnp.where(lane < SHARD, own, other)
     for part in range(ROWS // 128):
         ids = jnp.zeros((8, 128), jnp.int32)
         for h in (0, 1):
@@ -222,7 +242,9 @@
                         off = pos % 128
                         inside = (lane >= off) & (lane < off + HALF)
                         ids = jnp.where(inside, number * SHARD + h * HALF + lane - off, ids)
-        cid[:, part * 128:(part + 1) * 128] = ids
+                        rows = lax.broadcasted_iota(jnp.int32, (HALF, 128), 0)
+                        rid_t[pos:pos + HALF, :] = number * SHARD + h * HALF + rows
+        cid_t[:, part * 128:(part + 1) * 128] = ids
     acc[...] = jnp.zeros_like(acc)
 
     pass_t(0, 0, 1)
@@ -243,24 +265,30 @@
     pass_z(2, 0)
     landed(2 * SHARD, sr.at[1])
     split_i(128, 384)
-    block(0, 384, 0, 256, True, True)
     pass_t(1, 0, 1)
-    pass_z(2, 1)
-    share(2, 6)
     pass_t(1, 1, 1)
+    split_t(256, 512)
+
+    def nothing():
+        pass
+
+    def take_2():
+        pass_z(2, 1)
+        share(2, 6)
+
+    def take_4():
+        landed(2 * HALF, zr.at[6])
+        share(4)
+
+    block(0, 384, 0, 512, True, True, hooks=(take_2, nothing, lambda: pass_t(1, 3, 1)))
+    pass_z(3, 0)
     landed(2 * SHARD, sr.at[2])
     split_i(384, 640)
-    pass_t(1, 3, 1)
-    pass_z(3, 0)
-    block(384, 640, 0, 256, True, False)
-    pass_t(1, 2, 1)
-    split_t(256, 768)
+    block(384, 640, 0, 512, True, hooks=(nothing, lambda: pass_t(1, 2, 1)))
     pass_z(3, 1)
     share(3, 5)
-    block(0, 384, 256, 768, False, True)
-    landed(2 * HALF, zr.at[6])
-    share(4)
-    block(384, 640, 256, 768, False, False)
+    split_t(512, 768)
+    block(0, 640, 512, 768, False, True, across=True, hooks=(nothing, nothing, take_4))
     for p in (0, 1, 3, 2):
         pass_t(1, p, 2)
     split_t(768, 1024)
@@ -335,35 +363,39 @@
             total = total + sum_got[k]
         sum_own[stage + 1] = total
 
-    block(0, 512, 768, 1024, False, True)
-    block(512, 640, 768, 1024, False, False)
-    block(640, 1024, 768, 1024, True, False)
-    for p in (2, 1, 3, 0):
-        for h, d in HD:
-            go(RT[h, 1, p, 2, d])
-    block(896, 1024, 0, 768, False, False)
-    go(RS[4])
-    block(640, 896, 0, 256, False, False)
-    landed(SHARD, rsr.at[0])
-    add_s(4)
-    for d in (0, 1):
-        go(RZ[4, d, d])
-    block(640, 896, 256, 768, False, False)
+    d_img[640:1024, :] = jnp.zeros((384, D), F32)
+
+    def send_far():
+        for p in (2, 1, 3, 0):
+            for h, d in HD:
+                go(RT[h, 1, p, 2, d])
+
+    block(0, 1024, 768, 1024, False, True, across=True, hooks=(nothing, nothing, send_far))
+    block(896, 1024, 0, 768, hooks=(nothing, nothing, lambda: go(RS[4])))
+
+    def start_z():
+        landed(SHARD, rsr.at[0])
+        add_s(4)
+        for d in (0, 1):
+            go(RZ[4, d, d])
+
+    def near_t():
+        for p in (2, 1, 3, 0):
+            back_t(1, p, 2, (1, p, 1))
+
+    block(640, 896, 0, 768, flip=True, hooks=(start_z, nothing, near_t))
     for r in (3, 5, 2, 6, 1, 7, 0):
         go(RS[r])
     for k in range(3):
         sum_own[0, k:k + 1, :] = jnp.sum(acc[k], axis=0, keepdims=True)
     sum_own[0, 3:8, :] = jnp.zeros((5, 128), F32)
     fan(0)
-    back_t(1, 2, 2, (1, 2, 1))
     landed(2 * SHARD, rsr.at[1])
     for r in (3, 5):
         add_s(r)
     for d in (0, 1):
         go(RZ[3, d, 1 - d])
     back_z(4, 0)
-    for p in (1, 3, 0):
-        back_t(1, p, 2, (1, p, 1))
     landed(5 * SHARD, rsr.at[2])
     for r in (2, 6, 1, 7, 0):
         add_s(r)
@@ -420,7 +452,8 @@
         scratch_shapes=[
             big, big, split, split, split, split, eighth, eighth, eighth, eighth, big, big,
             pltpu.VMEM((ROWS, ROWS), F32), pltpu.VMEM((ROWS, ROWS), BF16), pltpu.VMEM((ROWS, ROWS), F8), pltpu.VMEM((ROWS, ROWS), F8),
-            pltpu.VMEM((ROWS, 128), jnp.int32), pltpu.VMEM((8, ROWS), jnp.int32), pltpu.VMEM((3, 8, 128), F32),
+            pltpu.VMEM((ROWS, 128), jnp.int32), pltpu.VMEM((8, ROWS), jnp.int32), pltpu.VMEM((ROWS, 128), jnp.int32),
+            pltpu.VMEM((8, ROWS), jnp.int32), pltpu.VMEM((3, 8, 128), F32),
             pltpu.VMEM((NZ, SHARD, D), F32), pltpu.VMEM((4, 2, SHARD, D), F32), pltpu.VMEM((40, HALF, D), F32),
             pltpu.VMEM((5, 8, 128), F32), pltpu.VMEM((14, 8, 128), F32),
             dma((7,)), dma((4,)), dma((10,)), dma((7,)), dma((3,)), dma((10,)), dma((4,)), dma((4,)),

time: 90.8 us -> 85.2 us (0.938)
  Pallas kernels: 88.7 us -> 83.1 us
    pallas_call x1, Pallas kernels: 86.8 us -> 81.2 us  [body(): pl.pallas_call(kernel, out_shape=[jax.ShapeDtypeStruct((8, 128), F32), sh...]
where the time goes in v3:
time: 85.2 us; the launch traced here: 85 us
  Pallas kernels  83.1 us (98%)
  between operations  1.93 us (2%)
    pallas_call x1, Pallas kernels, body(): pl.pallas_call(kernel, out_shape=[jax.ShapeDtypeStruct((8, 128), F32), sh...  81.2 us
    pallas_call x1, Pallas kernels, body(): pl.pallas_call(finish, out_shape=[one, shard, shard, one, one], in_specs=...  1.9 us

profile of v3, /device:TPU:1, one launch (start us, length us, event | category | flops | bytes accessed | tf_op | source)
XLA Modules:
  0.0 85.0 jit_solution(6929396473272998086)
XLA Ops:
  1.9 81.2 %shard_map.83 = (f32[8,128]{1,0:T(8,128)}, f32[64,1152]{1,0:T(8,128)}, f32[64,1152]{1,0:T(8,128)}) custom-call(f32[64,1152]{1,0:T(8,128)} %pic.1, f32[64,1152]{1,0:T(8,128)} %cap.1, f32[1]{0:T(128)S(6)} %copy.9.warmth, f32[1]{0:T(128)S(6)} %copy.10.bias), custom_call_target="tpu_custom_call" | custom-call | tf_op jit(solution)/shard_map/pallas_call | solution.py:447
  83.1 1.9 %shard_map.84 = (f32[1,1]{1,0:T(1,128)}, f32[64,1152]{1,0:T(8,128)}, f32[64,1152]{1,0:T(8,128)}, f32[1,1]{1,0:T(1,128)}, f32[1,1]{1,0:T(1,128)}) custom-call(f32[8,128]{1,0:T(8,128)} %get-tuple-element.13.sums, f32[64,1152]{1,0:T(8,128)} %get-tuple-element.14.pic, f32[64,1152]{1,0:T(8,128)} %get-tuple-element.15.cap), custom_call_target="tpu_custom_call" | custom-call | tf_op jit(solution)/shard_map/pallas_call | solution.py:463

commit v4 on v3

--- a/solution.py
+++ b/solution.py
@@ -13,8 +13,8 @@
 NX, NY, NZ = 4, 4, 8
 SHARD, HALF, QUARTER, D = 64, 32, 16, 1152
 ROWS = 1024
-SHARE = {0: 0, 1: 1, 7: 1, 2: 2, 6: 2, 3: 3, 5: 3, 4: 3}
-BACK = {4: 0, 3: 1, 5: 1, 2: 2, 6: 2, 1: 2, 7: 2, 0: 2}
+SHARE = {0: 0, 1: 1, 7: 1, 2: 2, 6: 2, 3: 3, 5: 3, 4: 4}
+BACK = {4: 0, 5: 0, 3: 1, 6: 1, 2: 2, 1: 2, 7: 2, 0: 2}
 NT = (((1,), (1,)), ((), ()))
 NN = (((1,), (0,)), ((), ()))
 TN = (((0,), (0,)), ((), ()))
@@ -62,7 +62,10 @@
 
 def kernel(pic, cap, warmth, bias, o_sum, o_pic, o_cap,
            img, txt, ih, il, th, tl, ih8, il8, th8, tl8, d_img, d_txt, s_ref, sh_ref, sh8_ref, sl8_ref, rid_i, cid_i, rid_t, cid_t, acc,
-           got_s, got_z, got_t, sum_own, sum_got, zr, sr, tr, rzr, rsr, rtr, qr, sent):
+           got_s, got_z, got_t, sum_own, sum_got, pic_own, cap_own, load, zr, sr, tr, rzr, rsr, rtr, qr, sent):
+    loads = [pltpu.make_async_copy(src, dst, load.at[k]) for k, (src, dst) in enumerate(((pic, pic_own), (cap, cap_own)))]
+    for copy in loads:
+        copy.start()
     im = lax.axis_index("img")
     tx = lax.axis_index("txt")
     z, x = im // NX, im % NX
@@ -77,8 +80,10 @@
     for other in others:
         pl.semaphore_signal(barrier, inc=1, device_id=other, device_id_type=MESH)
 
-    pic_unit, pic_norm = unit_rows(pic[...])
-    cap_unit, cap_norm = unit_rows(cap[...])
+    for copy in loads:
+        copy.wait()
+    pic_unit, pic_norm = unit_rows(pic_own[...])
+    cap_unit, cap_norm = unit_rows(cap_own[...])
     own_i = image_row(0, 0)
     img[own_i:own_i + SHARD, :] = pic_unit
     for h in (0, 1):
@@ -272,28 +277,31 @@
     def nothing():
         pass
 
-    def take_2():
-        pass_z(2, 1)
-        share(2, 6)
+    def take(s, n, *rs):
+        def hook():
+            pass_z(s, n)
+            share(*rs)
+
+        return hook
 
     def take_4():
         landed(2 * HALF, zr.at[6])
         share(4)
 
-    block(0, 384, 0, 512, True, True, hooks=(take_2, nothing, lambda: pass_t(1, 3, 1)))
-    pass_z(3, 0)
+    block(0, 256, 0, 512, True, True, hooks=(take(2, 1, 2, 6), nothing, lambda: pass_t(1, 3, 1)))
     landed(2 * SHARD, sr.at[2])
     split_i(384, 640)
-    block(384, 640, 0, 512, True, hooks=(nothing, lambda: pass_t(1, 2, 1)))
-    pass_z(3, 1)
-    share(3, 5)
+    block(256, 512, 0, 512, True, hooks=(take(3, 0), nothing, lambda: pass_t(1, 2, 1)))
     split_t(512, 768)
-    block(0, 640, 512, 768, False, True, across=True, hooks=(nothing, nothing, take_4))
+    block(0, 512, 512, 768, False, True, across=True, hooks=(take(3, 1, 3, 5),))
+    landed(2 * SHARD, sr.at[3])
+    split_i(640, 896)
+    block(512, 768, 0, 512, True, hooks=(nothing, take_4))
     for p in (0, 1, 3, 2):
         pass_t(1, p, 2)
     split_t(768, 1024)
-    landed(3 * SHARD, sr.at[3])
-    split_i(640, 1024)
+    landed(SHARD, sr.at[4])
+    split_i(896, 1024)
     for k, rows in enumerate((14 * HALF, NZ * SHARD, 15 * SHARD)):
         landed(rows, sent.at[k])
 
@@ -363,7 +371,7 @@
             total = total + sum_got[k]
         sum_own[stage + 1] = total
 
-    d_img[640:1024, :] = jnp.zeros((384, D), F32)
+    d_img[768:1024, :] = jnp.zeros((256, D), F32)
 
     def send_far():
         for p in (2, 1, 3, 0):
@@ -371,34 +379,41 @@
                 go(RT[h, 1, p, 2, d])
 
     block(0, 1024, 768, 1024, False, True, across=True, hooks=(nothing, nothing, send_far))
-    block(896, 1024, 0, 768, hooks=(nothing, nothing, lambda: go(RS[4])))
+    for r in (2, 1, 7, 0):
+        go(RS[r])
+
+    def send_back():
+        for r in (4, 5):
+            go(RS[r])
+
+    block(768, 1024, 0, 768, hooks=(nothing, nothing, send_back))
 
     def start_z():
-        landed(SHARD, rsr.at[0])
+        landed(2 * SHARD, rsr.at[0])
         add_s(4)
-        for d in (0, 1):
-            go(RZ[4, d, d])
+        add_s(5)
+        for k in ((4, 0, 0), (4, 1, 1), (3, 1, 0)):
+            go(RZ[k])
 
     def near_t():
         for p in (2, 1, 3, 0):
             back_t(1, p, 2, (1, p, 1))
 
-    block(640, 896, 0, 768, flip=True, hooks=(start_z, nothing, near_t))
-    for r in (3, 5, 2, 6, 1, 7, 0):
+    block(512, 768, 512, 768, flip=True, hooks=(start_z, nothing, near_t))
+    for r in (3, 6):
         go(RS[r])
     for k in range(3):
         sum_own[0, k:k + 1, :] = jnp.sum(acc[k], axis=0, keepdims=True)
     sum_own[0, 3:8, :] = jnp.zeros((5, 128), F32)
     fan(0)
+    landed(4 * SHARD, rsr.at[2])
+    for r in (2, 1, 7, 0):
+        add_s(r)
     landed(2 * SHARD, rsr.at[1])
-    for r in (3, 5):
+    for r in (3, 6):
         add_s(r)
-    for d in (0, 1):
-        go(RZ[3, d, 1 - d])
+    go(RZ[3, 0, 1])
     back_z(4, 0)
-    landed(5 * SHARD, rsr.at[2])
-    for r in (2, 6, 1, 7, 0):
-        add_s(r)
     fold(0)
     fan(1)
     back_z(3, 0)
@@ -440,14 +455,14 @@
 
 
 def body(picture_vectors, caption_vectors, warmth_exponent, offset_weight):
-    vmem, smem = pl.BlockSpec(memory_space=pltpu.VMEM), pl.BlockSpec(memory_space=pltpu.SMEM)
+    vmem, smem, hbm = (pl.BlockSpec(memory_space=m) for m in (pltpu.VMEM, pltpu.SMEM, pl.ANY))
     dma = pltpu.SemaphoreType.DMA
     big, split, eighth = pltpu.VMEM((ROWS, D), F32), pltpu.VMEM((ROWS, D), BF16), pltpu.VMEM((ROWS, D), F8)
     one, shard = jax.ShapeDtypeStruct((1, 1), F32), jax.ShapeDtypeStruct((SHARD, D), F32)
     results = pl.pallas_call(
         kernel,
         out_shape=[jax.ShapeDtypeStruct((8, 128), F32), shard, shard],
-        in_specs=[vmem, vmem, smem, smem],
+        in_specs=[hbm, hbm, smem, smem],
         out_specs=[vmem] * 3,
         scratch_shapes=[
             big, big, split, split, split, split, eighth, eighth, eighth, eighth, big, big,
@@ -455,8 +470,8 @@
             pltpu.VMEM((ROWS, 128), jnp.int32), pltpu.VMEM((8, ROWS), jnp.int32), pltpu.VMEM((ROWS, 128), jnp.int32),
             pltpu.VMEM((8, ROWS), jnp.int32), pltpu.VMEM((3, 8, 128), F32),
             pltpu.VMEM((NZ, SHARD, D), F32), pltpu.VMEM((4, 2, SHARD, D), F32), pltpu.VMEM((40, HALF, D), F32),
-            pltpu.VMEM((5, 8, 128), F32), pltpu.VMEM((14, 8, 128), F32),
-            dma((7,)), dma((4,)), dma((10,)), dma((7,)), dma((3,)), dma((10,)), dma((4,)), dma((4,)),
+            pltpu.VMEM((5, 8, 128), F32), pltpu.VMEM((14, 8, 128), F32), pltpu.VMEM((SHARD, D), F32), pltpu.VMEM((SHARD, D), F32), dma((2,)),
+            dma((7,)), dma((5,)), dma((10,)), dma((7,)), dma((3,)), dma((10,)), dma((4,)), dma((4,)),
         ],
         compiler_params=pltpu.CompilerParams(collective_id=0, has_side_effects=True, vmem_limit_bytes=62 * 2**20),
     )(picture_vectors, caption_vectors, warmth_exponent, offset_weight)

time: 85.2 us -> 83.2 us (0.977)
  Pallas kernels: 83.1 us -> 81.1 us
    pallas_call x1, Pallas kernels: 81.2 us -> 79.2 us  [body(): pl.pallas_call(kernel, out_shape=[jax.ShapeDtypeStruct((8, 128), F32), sh...]
where the time goes in v4:
time: 83.2 us; the launch traced here: 83 us
  Pallas kernels  81.1 us (97%)
  between operations  1.93 us (2%)
    pallas_call x1, Pallas kernels, body(): pl.pallas_call(kernel, out_shape=[jax.ShapeDtypeStruct((8, 128), F32), sh...  79.2 us
    pallas_call x1, Pallas kernels, body(): pl.pallas_call(finish, out_shape=[one, shard, shard, one, one], in_specs=...  1.9 us

profile of v4, /device:TPU:1, one launch (start us, length us, event | category | flops | bytes accessed | tf_op | source)
XLA Modules:
  0.0 83.0 jit_solution(7875582136239860088)
XLA Ops:
  1.9 79.2 %shard_map.83 = (f32[8,128]{1,0:T(8,128)}, f32[64,1152]{1,0:T(8,128)}, f32[64,1152]{1,0:T(8,128)}) custom-call(f32[64,1152]{1,0:T(8,128)} %pic.1, f32[64,1152]{1,0:T(8,128)} %cap.1, f32[1]{0:T(128)S(6)} %copy.9.warmth, f32[1]{0:T(128)S(6)} %copy.10.bias), custom_call_target="tpu_custom_call" | custom-call | tf_op jit(solution)/shard_map/pallas_call | solution.py:462
  81.1 1.9 %shard_map.84 = (f32[1,1]{1,0:T(1,128)}, f32[64,1152]{1,0:T(8,128)}, f32[64,1152]{1,0:T(8,128)}, f32[1,1]{1,0:T(1,128)}, f32[1,1]{1,0:T(1,128)}) custom-call(f32[8,128]{1,0:T(8,128)} %get-tuple-element.13.sums, f32[64,1152]{1,0:T(8,128)} %get-tuple-element.14.pic, f32[64,1152]{1,0:T(8,128)} %get-tuple-element.15.cap), custom_call_target="tpu_custom_call" | custom-call | tf_op jit(solution)/shard_map/pallas_call | solution.py:478

commit v5 on v4

--- a/solution.py
+++ b/solution.py
@@ -293,10 +293,9 @@
     split_i(384, 640)
     block(256, 512, 0, 512, True, hooks=(take(3, 0), nothing, lambda: pass_t(1, 2, 1)))
     split_t(512, 768)
-    block(0, 512, 512, 768, False, True, across=True, hooks=(take(3, 1, 3, 5),))
+    block(0, 512, 512, 768, False, True, across=True, hooks=(take(3, 1, 3, 5), nothing, take_4))
     landed(2 * SHARD, sr.at[3])
     split_i(640, 896)
-    block(512, 768, 0, 512, True, hooks=(nothing, take_4))
     for p in (0, 1, 3, 2):
         pass_t(1, p, 2)
     split_t(768, 1024)
@@ -371,7 +370,7 @@
             total = total + sum_got[k]
         sum_own[stage + 1] = total
 
-    d_img[768:1024, :] = jnp.zeros((256, D), F32)
+    d_img[512:1024, :] = jnp.zeros((512, D), F32)
 
     def send_far():
         for p in (2, 1, 3, 0):
@@ -399,7 +398,7 @@
         for p in (2, 1, 3, 0):
             back_t(1, p, 2, (1, p, 1))
 
-    block(512, 768, 512, 768, flip=True, hooks=(start_z, nothing, near_t))
+    block(512, 768, 0, 768, flip=True, hooks=(start_z, nothing, near_t))
     for r in (3, 6):
         go(RS[r])
     for k in range(3):

time: 83.2 us -> 83.3 us (level)
  no operation moved by 1% of the time
where the time goes in v5:
time: 83.3 us; the launch traced here: 83.1 us
  Pallas kernels  81.2 us (97%)
  between operations  1.93 us (2%)
    pallas_call x1, Pallas kernels, body(): pl.pallas_call(kernel, out_shape=[jax.ShapeDtypeStruct((8, 128), F32), sh...  79.3 us
    pallas_call x1, Pallas kernels, body(): pl.pallas_call(finish, out_shape=[one, shard, shard, one, one], in_specs=...  1.9 us

profile of v5, /device:TPU:1, one launch (start us, length us, event | category | flops | bytes accessed | tf_op | source)
XLA Modules:
  0.0 83.1 jit_solution(8769431091064445093)
XLA Ops:
  1.9 79.3 %shard_map.83 = (f32[8,128]{1,0:T(8,128)}, f32[64,1152]{1,0:T(8,128)}, f32[64,1152]{1,0:T(8,128)}) custom-call(f32[64,1152]{1,0:T(8,128)} %pic.1, f32[64,1152]{1,0:T(8,128)} %cap.1, f32[1]{0:T(128)S(6)} %copy.9.warmth, f32[1]{0:T(128)S(6)} %copy.10.bias), custom_call_target="tpu_custom_call" | custom-call | tf_op jit(solution)/shard_map/pallas_call | solution.py:461
  81.2 1.9 %shard_map.84 = (f32[1,1]{1,0:T(1,128)}, f32[64,1152]{1,0:T(8,128)}, f32[64,1152]{1,0:T(8,128)}, f32[1,1]{1,0:T(1,128)}, f32[1,1]{1,0:T(1,128)}) custom-call(f32[8,128]{1,0:T(8,128)} %get-tuple-element.13.sums, f32[64,1152]{1,0:T(8,128)} %get-tuple-element.14.pic, f32[64,1152]{1,0:T(8,128)} %get-tuple-element.15.cap), custom_call_target="tpu_custom_call" | custom-call | tf_op jit(solution)/shard_map/pallas_call | solution.py:477

commit v6 on v5

--- a/solution.py
+++ b/solution.py
@@ -50,14 +50,12 @@
 
 def pair_terms(scores, same, temperature, offset):
     logits = temperature * scores + offset
-    e = jnp.exp(logits)
-    u = 1.0 + e
-    r = 1.0 / u
-    slopes = jnp.where(same, -r, e * r)
-    g = jnp.where(same, 1.0 / e, e)
+    g = jnp.exp(jnp.where(same, -logits, logits))
+    u = 1.0 + g
+    r = pl.reciprocal(u, approx=True)
+    part = g * (r * (2.0 - u * r))
     small = g * (1.0 - g * (0.5 - g * (1.0 / 3.0)))
-    losses = jnp.where(g < 0.015625, small, jnp.log(1.0 + g))
-    return losses, slopes
+    return jnp.where(g < 0.015625, small, jnp.log(u)), jnp.where(same, -part, part)
 
 
 def kernel(pic, cap, warmth, bias, o_sum, o_pic, o_cap,
@@ -395,44 +393,46 @@
             go(RZ[k])
 
     def near_t():
-        for p in (2, 1, 3, 0):
+        for p in (2, 1, 3):
             back_t(1, p, 2, (1, p, 1))
 
-    block(512, 768, 0, 768, flip=True, hooks=(start_z, nothing, near_t))
-    for r in (3, 6):
-        go(RS[r])
+    def send_next():
+        for r in (3, 6):
+            go(RS[r])
+
+    block(512, 768, 0, 768, hooks=(start_z, nothing, send_next))
+    near_t()
     for k in range(3):
         sum_own[0, k:k + 1, :] = jnp.sum(acc[k], axis=0, keepdims=True)
     sum_own[0, 3:8, :] = jnp.zeros((5, 128), F32)
     fan(0)
-    landed(4 * SHARD, rsr.at[2])
-    for r in (2, 1, 7, 0):
-        add_s(r)
     landed(2 * SHARD, rsr.at[1])
     for r in (3, 6):
         add_s(r)
     go(RZ[3, 0, 1])
     back_z(4, 0)
+    landed(4 * SHARD, rsr.at[2])
+    for r in (2, 1, 7, 0):
+        add_s(r)
     fold(0)
     fan(1)
-    back_z(3, 0)
     back_t(1, 2, 1)
     for h, d in HD:
         go(RT[h, 0, 0, 2, d])
-    back_z(3, 1)
+    back_t(1, 0, 2, (1, 0, 1))
+    back_z(3, 0)
     fold(1)
     fan(2)
     back_t(1, 1, 1)
-    back_z(2, 0)
+    back_z(3, 1)
+    fold(2)
+    fan(3)
     back_t(1, 3, 1)
     back_t(0, 0, 2, (0, 0, 1))
+    back_z(2, 0)
     back_z(2, 1)
-    fold(2)
-    fan(3)
+    back_t(1, 0, 1)
     back_z(1, 0)
-    back_t(1, 0, 1)
-    back_z(1, 1)
-    o_pic[...] = project_back(pic_unit, pic_norm, warm_down * d_img[own_i:own_i + SHARD, :])
     fold(3)
     totals = jnp.sum(sum_own[4], axis=1, keepdims=True) * (1.0 / 16384.0)
     kind = lax.broadcasted_iota(jnp.int32, (8, 1), 0)
@@ -440,6 +440,8 @@
     back_t(0, 0, 1)
     grads = jnp.concatenate([d_txt[text_row(h, 0, 0):text_row(h, 0, 0) + HALF, :] for h in (0, 1)], 0)
     o_cap[...] = project_back(cap_unit, cap_norm, warm_down * grads)
+    back_z(1, 1)
+    o_pic[...] = project_back(pic_unit, pic_norm, warm_down * d_img[own_i:own_i + SHARD, :])
     for k, rows in enumerate((14 * HALF, NZ * SHARD, 15 * SHARD)):
         landed(rows, sent.at[k])
     pltpu.make_async_copy(sum_got, sum_got, sent.at[3]).wait()

time: 83.3 us -> 84.5 us (1.014)
  Pallas kernels: 81.2 us -> 82.4 us
    pallas_call x1, Pallas kernels: 79.3 us -> 80.5 us  [body(): pl.pallas_call(kernel, out_shape=[jax.ShapeDtypeStruct((8, 128), F32), sh...]
where the time goes in v6:
time: 84.5 us; the launch traced here: 84.4 us
  Pallas kernels  82.4 us (98%)
  between operations  1.93 us (2%)
    pallas_call x1, Pallas kernels, body(): pl.pallas_call(kernel, out_shape=[jax.ShapeDtypeStruct((8, 128), F32), sh...  80.5 us
    pallas_call x1, Pallas kernels, body(): pl.pallas_call(finish, out_shape=[one, shard, shard, one, one], in_specs=...  1.9 us

profile of v6, /device:TPU:1, one launch (start us, length us, event | category | flops | bytes accessed | tf_op | source)
XLA Modules:
  0.0 84.4 jit_solution(8300033365969858477)
XLA Ops:
  1.9 80.5 %shard_map.83 = (f32[8,128]{1,0:T(8,128)}, f32[64,1152]{1,0:T(8,128)}, f32[64,1152]{1,0:T(8,128)}) custom-call(f32[64,1152]{1,0:T(8,128)} %pic.1, f32[64,1152]{1,0:T(8,128)} %cap.1, f32[1]{0:T(128)S(6)} %copy.9.warmth, f32[1]{0:T(128)S(6)} %copy.10.bias), custom_call_target="tpu_custom_call" | custom-call | tf_op jit(solution)/shard_map/pallas_call | solution.py:463
  82.5 1.9 %shard_map.84 = (f32[1,1]{1,0:T(1,128)}, f32[64,1152]{1,0:T(8,128)}, f32[64,1152]{1,0:T(8,128)}, f32[1,1]{1,0:T(1,128)}, f32[1,1]{1,0:T(1,128)}) custom-call(f32[8,128]{1,0:T(8,128)} %get-tuple-element.13.sums, f32[64,1152]{1,0:T(8,128)} %get-tuple-element.14.pic, f32[64,1152]{1,0:T(8,128)} %get-tuple-element.15.cap), custom_call_target="tpu_custom_call" | custom-call | tf_op jit(solution)/shard_map/pallas_call | solution.py:479

commit v7 on v6

--- a/solution.py
+++ b/solution.py
@@ -50,12 +50,14 @@
 
 def pair_terms(scores, same, temperature, offset):
     logits = temperature * scores + offset
-    g = jnp.exp(jnp.where(same, -logits, logits))
-    u = 1.0 + g
-    r = pl.reciprocal(u, approx=True)
-    part = g * (r * (2.0 - u * r))
+    e = jnp.exp(logits)
+    u = 1.0 + e
+    r = 1.0 / u
+    slopes = jnp.where(same, -r, e * r)
+    g = jnp.where(same, 1.0 / e, e)
     small = g * (1.0 - g * (0.5 - g * (1.0 / 3.0)))
-    return jnp.where(g < 0.015625, small, jnp.log(u)), jnp.where(same, -part, part)
+    losses = jnp.where(g < 0.015625, small, jnp.log(1.0 + g))
+    return losses, slopes
 
 
 def kernel(pic, cap, warmth, bias, o_sum, o_pic, o_cap,
@@ -291,9 +293,10 @@
     split_i(384, 640)
     block(256, 512, 0, 512, True, hooks=(take(3, 0), nothing, lambda: pass_t(1, 2, 1)))
     split_t(512, 768)
-    block(0, 512, 512, 768, False, True, across=True, hooks=(take(3, 1, 3, 5), nothing, take_4))
+    block(0, 512, 512, 768, False, True, across=True, hooks=(take(3, 1, 3, 5),))
     landed(2 * SHARD, sr.at[3])
     split_i(640, 896)
+    block(512, 768, 0, 512, True, hooks=(nothing, take_4))
     for p in (0, 1, 3, 2):
         pass_t(1, p, 2)
     split_t(768, 1024)
@@ -368,7 +371,7 @@
             total = total + sum_got[k]
         sum_own[stage + 1] = total
 
-    d_img[512:1024, :] = jnp.zeros((512, D), F32)
+    d_img[768:1024, :] = jnp.zeros((256, D), F32)
 
     def send_far():
         for p in (2, 1, 3, 0):
@@ -396,12 +399,9 @@
         for p in (2, 1, 3):
             back_t(1, p, 2, (1, p, 1))
 
-    def send_next():
-        for r in (3, 6):
-            go(RS[r])
-
-    block(512, 768, 0, 768, hooks=(start_z, nothing, send_next))
-    near_t()
+    block(512, 768, 512, 768, flip=True, hooks=(start_z, nothing, near_t))
+    for r in (3, 6):
+        go(RS[r])
     for k in range(3):
         sum_own[0, k:k + 1, :] = jnp.sum(acc[k], axis=0, keepdims=True)
     sum_own[0, 3:8, :] = jnp.zeros((5, 128), F32)

time: 84.5 us -> 82.9 us (0.981)
  Pallas kernels: 82.4 us -> 80.8 us
    pallas_call x1, Pallas kernels: 80.5 us -> 78.9 us  [body(): pl.pallas_call(kernel, out_shape=[jax.ShapeDtypeStruct((8, 128), F32), sh...]
where the time goes in v7:
time: 82.9 us; the launch traced here: 82.8 us
  Pallas kernels  80.8 us (97%)
  between operations  1.93 us (2%)
    pallas_call x1, Pallas kernels, body(): pl.pallas_call(kernel, out_shape=[jax.ShapeDtypeStruct((8, 128), F32), sh...  78.9 us
    pallas_call x1, Pallas kernels, body(): pl.pallas_call(finish, out_shape=[one, shard, shard, one, one], in_specs=...  1.9 us

profile of v7, /device:TPU:1, one launch (start us, length us, event | category | flops | bytes accessed | tf_op | source)
XLA Modules:
  0.0 82.8 jit_solution(17370133386781839544)
XLA Ops:
  1.9 78.9 %shard_map.83 = (f32[8,128]{1,0:T(8,128)}, f32[64,1152]{1,0:T(8,128)}, f32[64,1152]{1,0:T(8,128)}) custom-call(f32[64,1152]{1,0:T(8,128)} %pic.1, f32[64,1152]{1,0:T(8,128)} %cap.1, f32[1]{0:T(128)S(6)} %copy.9.warmth, f32[1]{0:T(128)S(6)} %copy.10.bias), custom_call_target="tpu_custom_call" | custom-call | tf_op jit(solution)/shard_map/pallas_call | solution.py:463
  80.9 1.9 %shard_map.84 = (f32[1,1]{1,0:T(1,128)}, f32[64,1152]{1,0:T(8,128)}, f32[64,1152]{1,0:T(8,128)}, f32[1,1]{1,0:T(1,128)}, f32[1,1]{1,0:T(1,128)}) custom-call(f32[8,128]{1,0:T(8,128)} %get-tuple-element.13.sums, f32[64,1152]{1,0:T(8,128)} %get-tuple-element.14.pic, f32[64,1152]{1,0:T(8,128)} %get-tuple-element.15.cap), custom_call_target="tpu_custom_call" | custom-call | tf_op jit(solution)/shard_map/pallas_call | solution.py:479
